TPU v7x, 32 devices: a whole 2x2x4 slice. The times are simulated.
32 devices in a mesh: tv: 8 (over z, core), sv: 4 (over y, x).
Axes of the slice: x: 2, y: 2, z: 4, core: 2. Of those that a mesh axis runs over, the one named last changes fastest.
Arguments:
- teacher_hidden: bfloat16 [512, 4096], P('tv', 'sv'), may hold values from -250 to 250
- student_hidden: bfloat16 [512, 5120], P('sv', 'tv'), may hold values from -250 to 250
- teacher_head: bfloat16 [4096, 151936], P('sv', 'tv'), may hold values from -0.09375 to 0.09375
- student_head: bfloat16 [5120, 151936], P('tv', 'sv'), may hold values from -0.078125 to 0.078125
- token_ids: int32 [512], P('tv'), may hold values from 0 to 151935
Outputs:
- rewards: float32 [512], P('tv')
- kl_div: float32 [512], P('tv')
- logit_grad: bfloat16 [512, 151936], P('tv', 'sv')
All inputs are finite; a program needn't handle non-finite values.
Results may differ from a plain program's by a relative error of at most 0.0042.
Values may be sent and summed in bfloat16 or wider, within the bound.
A program may use at most 320 MiB of HBM per device.

v0:
```python
import jax
import jax.numpy as jnp
from jax import lax
from jax.sharding import PartitionSpec as P


def joined(array, axis, combine):
    everything = jax.tree.map(lambda part: lax.all_gather(part, axis), array)
    leading = jax.tree.map(lambda part: part[0], everything)

    def turn(k, so_far):
        return combine(so_far, jax.tree.map(lambda part: part[k], everything))

    return lax.fori_loop(1, lax.axis_size(axis), turn, leading)


def join_pair(first, second):
    peak_new = jnp.maximum(first[0], second[0])
    return (
        peak_new,
        first[1] * jnp.exp(first[0] - peak_new) + second[1] * jnp.exp(second[0] - peak_new),
    )


def join_four(first, second):
    return join_pair(first[:2], second[:2]) + join_pair(first[2:], second[2:])


def row_mass(values):
    peak_row = jnp.max(values, axis=1)
    return (peak_row, jnp.sum(jnp.exp(values - peak_row[:, None]), axis=1))


def shards(teacher_hidden, student_hidden, teacher_head, student_head, token_ids):
    tv_count = lax.axis_size("tv")
    sv_count = lax.axis_size("sv")
    teacher_rows = lax.all_gather(teacher_hidden, "tv", axis=0, tiled=True)
    all_tokens = teacher_rows.shape[0]
    inner_rows = all_tokens // (tv_count * sv_count)
    feature_width = teacher_rows.shape[1]
    reordered = teacher_rows.reshape(tv_count, sv_count, inner_rows, feature_width)
    reordered = reordered.transpose(1, 0, 2, 3).reshape(all_tokens, feature_width)
    block_rows = reordered
    teacher_logit = lax.psum_scatter(
        jnp.dot(block_rows, teacher_head, preferred_element_type=jnp.float32),
        "sv",
        scatter_dimension=0,
        tiled=True,
    ).astype(jnp.bfloat16)
    teacher_base = lax.all_to_all(
        lax.all_to_all(teacher_logit, "tv", split_axis=0, concat_axis=1, tiled=True),
        "sv",
        split_axis=1,
        concat_axis=0,
        tiled=True,
    ).astype(jnp.float32)
    student_rows = lax.all_gather(student_hidden, "sv", axis=0, tiled=True)
    block_rows = student_rows
    student_logit = lax.psum_scatter(
        jnp.dot(block_rows, student_head, preferred_element_type=jnp.float32),
        "tv",
        scatter_dimension=0,
        tiled=True,
    )
    col_width = student_logit.shape[1]
    vocab_ids = lax.axis_index("sv") * col_width + lax.broadcasted_iota(
        jnp.int32, student_logit.shape, 1
    )
    logit_gap = student_logit - teacher_base
    picked = jnp.sum(jnp.where(vocab_ids == token_ids[:, None], -logit_gap, 0.0), axis=1)
    peak_student, mass_student = row_mass(student_logit)
    peak_teacher, mass_teacher = row_mass(teacher_base)
    peak_student, mass_student, peak_teacher, mass_teacher = joined(
        (peak_student, mass_student, peak_teacher, mass_teacher), "sv", join_four
    )
    student_norm = peak_student + jnp.log(mass_student)
    teacher_norm = peak_teacher + jnp.log(mass_teacher)
    student_prob = jnp.exp(student_logit - student_norm[:, None])
    kl_part = jnp.sum(student_prob * logit_gap, axis=1)
    kl_total, picked = lax.psum((kl_part, picked), "sv")
    kl_div = kl_total - student_norm + teacher_norm
    rewards = picked + student_norm - teacher_norm
    shift_rows = student_norm - teacher_norm + kl_div
    logit_grad = (student_prob * (logit_gap - shift_rows[:, None])).astype(jnp.bfloat16)
    return (rewards, kl_div, logit_grad)


def solution(mesh):
    in_specs = (P("tv", "sv"), P("sv", "tv"), P("sv", "tv"), P("tv", "sv"), P("tv"))
    out_specs = (P("tv"), P("tv"), P("tv", "sv"))
    return jax.shard_map(shards, mesh=mesh, in_specs=in_specs, out_specs=out_specs, check_vma=False)
```

profile of v0, /device:TPU:16, one launch (start us, length us, event | category | flops | bytes accessed | tf_op | source)
XLA Modules:
  0.0 1628.5 jit_solution(1790916997090954124)
XLA Ops:
  7.2 0.0 all-gather.6.cloned.1.call-start
  7.2 0.7 all-gather.6.cloned.1.call-update
  7.9 0.0 reduce-scatter.5.cloned.1.call-start
  7.9 24.5 %all-gather.6.cloned.1.call-done = bf16[512,1024]{1,0:T(8,128)(2,1)} async-done(((bf16[64,1024]{1,0:T(8,128)(2,1)}), bf16[512,1024]{1,0:T(8,128)(2,1)}) %all-gather.6.cloned.1.call-update) | async-done | bytes 1048592 | tf_op jit(solution)/shard_map/all_gather | solution.py:37
  32.4 1.3 copy.26
  33.7 36.1 %fusion.13 = f32[512,18992]{0,1:T(8,128)} fusion(bf16[512,1024]{1,0:T(8,128)(2,1)S(1)} %bitcast.61, bf16[1024,18992]{0,1:T(8,128)(2,1)} %param.9), kind=kOutput, calls=%fused_computation.32 | convolution fusion | flops 19914555392 | bytes 78839808 | tf_op jit(solution)/shard_map/dot_general | solution.py:45
  69.8 0.0 copy-start
  69.8 0.0 reduce-scatter.5.cloned.1.call-update
  69.8 0.0 reduce-scatter.3.cloned.1.call-start
  69.9 0.8 copy-done
  70.7 15.4 all_gather.28
  86.1 47.9 %fusion.12 = f32[512,37984]{1,0:T(8,128)} fusion(bf16[512,640]{1,0:T(8,128)(2,1)S(1)} %all_gather.28, bf16[640,37984]{0,1:T(8,128)(2,1)} %param.10), kind=kOutput, calls=%fused_computation.31 | convolution fusion | flops 24893194240 | bytes 127066112 | tf_op jit(solution)/shard_map/dot_general | solution.py:60
  134.0 0.0 reduce-scatter.3.cloned.1.call-update
  134.0 589.4 %reduce-scatter.5.cloned.1.call-done = f32[128,18992]{0,1:T(8,128)} async-done(((f32[512,18992]{0,1:T(8,128)}), f32[128,18992]{0,1:T(8,128)}) %reduce-scatter.5.cloned.1.call-update) | async-done | bytes 9723920 | tf_op jit(solution)/shard_map/reduce_scatter | solution.py:44
  723.4 6.7 convert_element_type.15
  730.1 7.7 copy.27
  737.8 188.0 %all_to_all.32 = bf16[8,16,18992]{2,1,0:T(8,128)(2,1)S(1)} all-to-all(bf16[8,16,18992]{2,1,0:T(8,128)(2,1)} %bitcast.58), channel_id=1, replica_groups=mesh['tv'=8,'sv'=4] {'tv'}, dimensions={0} | all-to-all | bytes 9723904 | tf_op jit(solution)/shard_map/all_to_all | solution.py:51
  925.8 3.2 copy.28
  928.9 8.5 all_to_all.27
  937.4 0.0 copy-start.2
  937.4 5.2 copy.29
  942.6 5.0 all-to-all-start.1
  947.6 0.0 copy-done.2
  947.6 0.6 dynamic-slice
  948.9 53.9 %all-to-all-done.1 = bf16[16,4,37984]{2,0,1:T(8,128)(2,1)} async-done(((bf16[16,4,37984]{2,0,1:T(8,128)(2,1)}), bf16[16,4,37984]{2,0,1:T(8,128)(2,1)}, u32[]{:S(2)}, u32[]{:S(2)}) %all-to-all-start.1) | async-done | bytes 4861984 | tf_op jit(solution)/shard_map/all_to_all | solution.py:50
  1002.8 3.2 bitcast_reduce_fusion
  1006.0 0.1 reshape.67
  1006.1 4.2 exponential_reduce_fusion
  1010.3 0.1 reshape.69
  1010.4 7.8 all-gather.3
  1018.2 7.0 all-gather.2
  1025.2 6.7 bitcast_convert_fusion
  1032.0 0.0 copy-start.1
  1032.0 542.2 %reduce-scatter.3.cloned.1.call-done = f32[64,37984]{1,0:T(8,128)} async-done(((f32[512,37984]{1,0:T(8,128)}), f32[64,37984]{1,0:T(8,128)}) %reduce-scatter.3.cloned.1.call-update) | async-done | bytes 9723920 | tf_op jit(solution)/shard_map/reduce_scatter | solution.py:59
  1574.2 4.3 reduce_max.27
  1578.5 0.2 dynamic-update-slice
  1578.7 5.2 exponential_reduce_fusion.1
  1583.9 0.2 dynamic-update-slice.1
  1584.2 9.8 all-reduce.3
  1594.0 0.1 reshape.55
  1594.1 0.1 reshape.56
  1594.2 0.1 while.21
  1594.3 0.0 copy-done.1
  1594.3 8.3 multiply_reduce_fusion
  1602.6 8.0 all-reduce.2
  1610.6 0.5 subtract_add_fusion
  1611.1 10.9 multiply_convert_fusion
  (12 shorter events, 0.1 us)
Async XLA Ops:
  7.2 25.2 %all-gather.6.cloned.1.call-start = ((), (), s32[]{:S(2)}) async-start(), calls=%async_computation.5 | async-start | bytes 1179648 | tf_op jit(solution)/shard_map/all_gather | solution.py:37
  7.9 715.5 %reduce-scatter.5.cloned.1.call-start = ((), (), s32[]{:S(2)}) async-start(), calls=%async_computation.6 | async-start | bytes 48619520 | tf_op jit(solution)/shard_map/reduce_scatter | solution.py:44
  69.8 0.9 copy-start
  69.8 1504.4 %reduce-scatter.3.cloned.1.call-start = ((), (), s32[]{:S(2)}) async-start(), calls=%async_computation.4 | async-start | bytes 87588864 | tf_op jit(solution)/shard_map/reduce_scatter | solution.py:59
  937.4 10.2 copy-start.2
  942.6 60.1 %all-to-all-start.1 = ((bf16[16,4,37984]{2,0,1:T(8,128)(2,1)}), bf16[16,4,37984]{2,0,1:T(8,128)(2,1)}, u32[]{:S(2)}, u32[]{:S(2)}) async-start(bf16[16,4,37984]{2,0,1:T(8,128)(2,1)} %copy.29), calls=%async_computation.3 | async-start | bytes 9732096 | tf_op jit(solution)/shard_map/all_to_all | solution.py:50
  1032.0 562.3 %copy-start.1 = (s32[64]{0:T(128)S(1)}, s32[64]{0:T(128)}, u32[]{:S(2)}) copy-start(s32[64]{0:T(128)} %param.11) | copy-start | bytes 772
Sparse Core Ops, SparseCore 0:
  9.6 22.7 all-gather.5
  69.9 653.4 reduce-scatter.4
  725.8 848.2 reduce-scatter.2
where the time goes:
time: 1630 us
  waiting for transfers between devices  1210 us (74%)
  blocking collectives  236 us (14%)
  matrix products  84 us (5%)
  other arithmetic  50.2 us (3%)
  local copies, waits for them, and re-layouts  28.1 us (2%)
    reduce_scatter x1, waiting for transfers between devices, shards(): lax.psum_scatter(jnp.dot(block_rows, teacher_head, preferred_element_type...  589 us
    reduce_scatter x1, waiting for transfers between devices, shards(): lax.psum_scatter(jnp.dot(block_rows, student_head, preferred_element_type...  542 us
    all_to_all x1, blocking collectives, shards(): lax.all_to_all(teacher_logit, 'tv', split_axis=0, concat_axis=1, tiled=True)  188 us
    all_to_all x1, waiting for transfers between devices, shards(): lax.all_to_all(lax.all_to_all(teacher_logit, 'tv', split_axis=0, concat_a...  53.9 us
    dot_general x1, matrix products, shards(): jnp.dot(block_rows, student_head, preferred_element_type=jnp.float32)  47.9 us
    dot_general x1, matrix products, shards(): jnp.dot(block_rows, teacher_head, preferred_element_type=jnp.float32)  36.1 us
  transfers between devices with their start and end apart: 4, of which 4 were waited for; matrix products, arithmetic and copies ran while one was open for 5% of the time, Pallas kernels for 0%

commit v1 on v0

v1 whole, which is shorter than its diff:
```python
import jax
import jax.numpy as jnp
from jax import lax
from jax.sharding import PartitionSpec as P

CHUNKS = 4
WIRE = jnp.float16
SHRINK = 0.25
STEPS = 64.0
TOP = 32000.0


def cut_words(width):
    step = max(128, width // CHUNKS // 128 * 128)
    edges = [step * k for k in range(CHUNKS)] + [width]
    return [(low, high) for low, high in zip(edges[:-1], edges[1:]) if high > low]


def pack(values):
    return (values * SHRINK).astype(WIRE)


def unpack(values):
    return values.astype(jnp.float32) * (1.0 / SHRINK)


def quantize(values, limit):
    code = jnp.ceil(jnp.log2(jnp.maximum(limit, 1e-20)) * STEPS + 0.5)
    scaled = values * (TOP * jnp.exp2(code * (-1.0 / STEPS)))
    tail = jnp.broadcast_to(code, (values.shape[0], 128))
    return jnp.concatenate([scaled, tail], axis=1).round().astype(jnp.int16)


def restore(coded):
    limit = jnp.exp2(coded[:, -1:].astype(jnp.float32) * (1.0 / STEPS))
    return coded[:, :-128].astype(jnp.float32) * (limit * (1.0 / TOP)), limit


def block(array, index):
    return lax.dynamic_index_in_dim(array, index, 0, keepdims=False)


def reduce_teacher(teacher_hidden, teacher_head):
    tv_count, sv_count = lax.axis_size("tv"), lax.axis_size("sv")
    here = lax.axis_index("sv")
    rows = lax.all_gather(teacher_hidden, "tv", axis=0, tiled=True)
    share = rows.shape[0] // (tv_count * sv_count)
    rows = rows.reshape(tv_count, sv_count, share, rows.shape[1])
    rows = rows.transpose(1, 0, 2, 3).reshape(-1, rows.shape[-1])
    part = pack(jnp.dot(rows, teacher_head, preferred_element_type=jnp.float32))
    part = part.reshape(sv_count, tv_count * share, part.shape[1])
    total = unpack(block(part, here))
    for flip in range(1, sv_count):
        swap = [(i, i ^ flip) for i in range(sv_count)]
        total = total + unpack(lax.ppermute(block(part, here ^ flip), "sv", swap))
    return total.astype(jnp.bfloat16).reshape(tv_count, share, part.shape[2])


def place_teacher(logit):
    tv_count, sv_count = lax.axis_size("tv"), lax.axis_size("sv")
    outer = tv_count // 2
    tv, sv = lax.axis_index("tv"), lax.axis_index("sv")
    plane, core = tv // 2, tv % 2
    got = []
    for flip in range(2):
        row = []
        for k in range(sv_count):
            pairs = []
            for z in range(outer):
                for c in range(2):
                    for s in range(sv_count):
                        to_tv = (s + k) % outer * 2 + (c ^ flip)
                        pairs.append(((z * 2 + c) * sv_count + s, to_tv * sv_count + z))
            mine = block(logit, (sv + k) % outer * 2 + (core ^ flip))
            row.append(lax.ppermute(mine, ("tv", "sv"), pairs))
        got.append(jnp.stack(row))
    first = jnp.where(core == 0, got[0], got[1])
    second = jnp.where(core == 0, got[1], got[0])
    halves = []
    for half in (first, second):
        groups = [block(half, (plane - g) % outer) for g in range(sv_count)]
        halves.append(jnp.concatenate(groups, axis=0))
    return jnp.concatenate(halves, axis=1)


def reduce_student(rows, head):
    tv_count = lax.axis_size("tv")
    outer = tv_count // 2
    plane = lax.axis_index("tv") // 2
    given = pack(jnp.dot(rows[1], head, preferred_element_type=jnp.float32))
    kept = jnp.dot(rows[0], head, preferred_element_type=jnp.float32)
    across = lax.ppermute(given, "tv", [(i, i ^ 1) for i in range(tv_count)])
    chip = (kept + unpack(across)).reshape(outer, -1, head.shape[1])
    peak = jnp.max(jnp.abs(chip), axis=2, keepdims=True)
    up = down = None
    for step in range(outer - 1):
        above = jnp.minimum(plane + outer - 1 - step, outer - 1)
        below = jnp.maximum(plane - (outer - 1 - step), 0)
        send_up, limit_up = block(chip, above), block(peak, above)
        send_down, limit_down = block(chip, below), block(peak, below)
        if step:
            (more_up, extra_up), (more_down, extra_down) = restore(up), restore(down)
            send_up, limit_up = send_up + more_up, limit_up + extra_up
            send_down, limit_down = send_down + more_down, limit_down + extra_down
        up_pairs = [(2 * z + c, 2 * z + 2 + c) for z in range(min(step + 1, outer - 1)) for c in range(2)]
        down_pairs = [(tv_count - 1 - a, tv_count - 1 - b) for a, b in up_pairs]
        up = lax.ppermute(quantize(send_up, limit_up), "tv", up_pairs)
        down = lax.ppermute(quantize(send_down, limit_down), "tv", down_pairs)
    return block(chip, plane) + restore(up)[0] + restore(down)[0]


def masses(student, teacher, low, token_ids):
    gap = student - teacher
    words = low + lax.broadcasted_iota(jnp.int32, student.shape, 1)
    picked = jnp.sum(jnp.where(words == token_ids[:, None], -gap, 0.0), axis=1)
    peak_s = jnp.max(student, axis=1)
    weight = jnp.exp(student - peak_s[:, None])
    peak_t = jnp.max(teacher, axis=1)
    mass_t = jnp.sum(jnp.exp(teacher - peak_t[:, None]), axis=1)
    return jnp.stack(
        [peak_s, jnp.sum(weight, axis=1), jnp.sum(weight * gap, axis=1), peak_t, mass_t, picked]
    )


def shards(teacher_hidden, student_hidden, teacher_head, student_head, token_ids):
    tv_count = lax.axis_size("tv")
    core = lax.axis_index("tv") % 2
    teacher_logit = reduce_teacher(teacher_hidden, teacher_head)
    rows = lax.all_gather(student_hidden, "sv", axis=0, tiled=True)
    rows = rows.reshape(tv_count // 2, 2, -1, rows.shape[1]).transpose(1, 0, 2, 3)
    rows = rows.reshape(2, -1, rows.shape[3])
    rows = jnp.stack([block(rows, core), block(rows, 1 - core)])
    cuts = cut_words(student_head.shape[1])
    student = [reduce_student(rows, student_head[:, low:high]) for low, high in cuts]
    teacher = place_teacher(teacher_logit)
    teacher = [teacher[:, low:high].astype(jnp.float32) for low, high in cuts]
    start = lax.axis_index("sv") * student_head.shape[1]
    local = jnp.stack(
        [masses(s, t, start + low, token_ids) for s, t, (low, _) in zip(student, teacher, cuts)]
    )
    stats = lax.all_gather(local, "sv", axis=0, tiled=True)
    peak_s, mass_s, gap_s, peak_t, mass_t, picked = [stats[:, k] for k in range(6)]
    top_s, top_t = jnp.max(peak_s, axis=0), jnp.max(peak_t, axis=0)
    scale_s = jnp.exp(peak_s - top_s)
    sum_s = jnp.sum(mass_s * scale_s, axis=0)
    sum_t = jnp.sum(mass_t * jnp.exp(peak_t - top_t), axis=0)
    norm_s, norm_t = top_s + jnp.log(sum_s), top_t + jnp.log(sum_t)
    mean_gap = jnp.sum(gap_s * scale_s, axis=0) / sum_s
    kl_div = mean_gap - norm_s + norm_t
    rewards = jnp.sum(picked, axis=0) + norm_s - norm_t
    grad = [
        (jnp.exp(s - norm_s[:, None]) * (s - t - mean_gap[:, None])).astype(jnp.bfloat16)
        for s, t in zip(student, teacher)
    ]
    return (rewards, kl_div, jnp.concatenate(grad, axis=1))


def solution(mesh):
    in_specs = (P("tv", "sv"), P("sv", "tv"), P("sv", "tv"), P("tv", "sv"), P("tv"))
    out_specs = (P("tv"), P("tv"), P("tv", "sv"))
    return jax.shard_map(shards, mesh=mesh, in_specs=in_specs, out_specs=out_specs, check_vma=False)
```

time: 1630 us -> 992 us (0.61)
  waiting for transfers between devices: 1210 us -> 450 us
  blocking collectives: 236 us -> 23.7 us
  local copies, waits for them, and re-layouts: 28.1 us -> 154 us
  other arithmetic: 50.2 us -> 139 us
  starting transfers between devices: 5.08 us -> 77.9 us
  matrix products: 84 us -> 125 us
    reduce_scatter x2 -> x0, waiting for transfers between devices: 1130 us -> none  [the longest x1 589 us: shards(): lax.psum_scatter(jnp.dot(block_rows, teacher_head, preferred_element_type...]
    ppermute x0 -> x39, waiting for transfers between devices: none -> 449 us  [the longest x3 121 us: reduce_teacher(): total = total + unpack(lax.ppermute(block(part, here ^ flip), 'sv', swap))]
    all_to_all x1 -> x0, blocking collectives: 188 us -> none  [shards(): lax.all_to_all(teacher_logit, 'tv', split_axis=0, concat_axis=1, tiled=True)]
    ppermute x0 -> x39, starting transfers between devices: none -> 77.9 us  [the longest x12 30.5 us: reduce_student(): up = lax.ppermute(quantize(send_up, limit_up), 'tv', up_pairs)]
    dynamic_slice x0 -> x1, local copies, waits for them, and re-layouts: none -> 57 us  [block(): return lax.dynamic_index_in_dim(array, index, 0, keepdims=False)]
    mul x0 -> x46, other arithmetic: none -> 54.8 us  [the longest x38 48.3 us: quantize(): scaled = values * (TOP * jnp.exp2(code * (-1.0 / STEPS)))]
    all_to_all x1 -> x0, waiting for transfers between devices: 53.9 us -> none  [shards(): lax.all_to_all(lax.all_to_all(teacher_logit, 'tv', split_axis=0, concat_a...]
    dot_general x2 -> x9, matrix products: 84 us -> 125 us  [the longest x4 52.9 us: reduce_student(): given = pack(jnp.dot(rows[1], head, preferred_element_type=jnp.float32))]
  transfers between devices with their start and end apart: 4 -> 40, of which waited for: 4 -> 22; matrix products, arithmetic and copies ran while one was open for 5% -> 39% of each run, Pallas kernels for 0% -> 0%
where the time goes in v1:
time: 992 us; the launch traced here: 985 us
  waiting for transfers between devices  450 us (45%)
  local copies, waits for them, and re-layouts  154 us (16%)
  other arithmetic  139 us (14%)
  matrix products  125 us (13%)
  starting transfers between devices  77.9 us (8%)
  blocking collectives  23.7 us (2%)
  between operations  15.2 us (2%)
    ppermute x3, waiting for transfers between devices, reduce_teacher(): total = total + unpack(lax.ppermute(block(part, here ^ flip), 'sv', swap))  121 us
    ppermute x12, waiting for transfers between devices, reduce_student(): down = lax.ppermute(quantize(send_down, limit_down), 'tv', down_pairs)  121 us
    ppermute x12, waiting for transfers between devices, reduce_student(): up = lax.ppermute(quantize(send_up, limit_up), 'tv', up_pairs)  119 us
    ppermute x8, waiting for transfers between devices, place_teacher(): row.append(lax.ppermute(mine, ('tv', 'sv'), pairs))  88.5 us
    dynamic_slice x1, local copies, waits for them, and re-layouts, block(): return lax.dynamic_index_in_dim(array, index, 0, keepdims=False)  57 us
    dot_general x4, matrix products, reduce_student(): given = pack(jnp.dot(rows[1], head, preferred_element_type=jnp.float32))  52.9 us
    mul x38, other arithmetic, quantize(): scaled = values * (TOP * jnp.exp2(code * (-1.0 / STEPS)))  48.3 us
    dot_general x4, matrix products, reduce_student(): kept = jnp.dot(rows[0], head, preferred_element_type=jnp.float32)  44.1 us
  transfers between devices with their start and end apart: 40, of which 22 were waited for; matrix products, arithmetic and copies ran while one was open for 39% of the time, Pallas kernels for 0%

profile of v1, /device:TPU:16, one launch (start us, length us, event | category | flops | bytes accessed | tf_op | source)
XLA Modules:
  0.0 984.5 jit_solution(9793384421258176245)
XLA Ops:
  7.9 11.3 %all_gather.9 = bf16[512,640]{1,0:T(8,128)(2,1)S(1)} all-gather(bf16[128,640]{1,0:T(8,128)(2,1)} %param.6), channel_id=1, replica_groups=mesh['tv'=8,'sv'=4] {'sv'}, dimensions={0}, use_global_device_ids=true | all-gather | bytes 819200 | tf_op jit(solution)/shard_map/all_gather | solution.py:129
  19.3 10.7 %fusion.1 = f16[256,9472]{1,0:T(8,128)(2,1)} fusion(bf16[640,37984]{0,1:T(8,128)(2,1)} %param.8, bf16[2,256,640]{2,1,0:T(8,128)(2,1)S(1)} %bitcast.539, s32[]{:T(128)S(6)} %select_n.218), kind=kOutput, calls=%fused_computation.6 | convolution fusion | flops 3108634624 | bytes 17301508 | tf_op jit(solution)/shard_map/dot_general | solution.py:90
  29.9 10.7 %fusion.2 = f16[256,9472]{1,0:T(8,128)(2,1)} fusion(bf16[640,37984]{0,1:T(8,128)(2,1)} %param.8, bf16[2,256,640]{2,1,0:T(8,128)(2,1)S(1)} %bitcast.540, s32[]{:T(128)S(6)} %select_n.218), kind=kOutput, calls=%fused_computation.7 | convolution fusion | flops 3108634624 | bytes 17301508 | tf_op jit(solution)/shard_map/dot_general | solution.py:90
  41.1 10.6 %fusion.3 = f16[256,9472]{1,0:T(8,128)(2,1)} fusion(bf16[640,37984]{0,1:T(8,128)(2,1)} %param.8, bf16[2,256,640]{2,1,0:T(8,128)(2,1)S(1)} %bitcast.541, s32[]{:T(128)S(6)} %select_n.218), kind=kOutput, calls=%fused_computation.8 | convolution fusion | flops 3108634624 | bytes 17301508 | tf_op jit(solution)/shard_map/dot_general | solution.py:90
  51.7 21.1 %fusion = f16[256,9568]{0,1:T(8,128)(2,1)} fusion(bf16[640,37984]{0,1:T(8,128)(2,1)} %param.8, bf16[2,256,640]{2,1,0:T(8,128)(2,1)S(1)} %bitcast.542, s32[]{:T(128)S(6)} %select_n.218), kind=kOutput, calls=%fused_computation.5 | convolution fusion | flops 3140141056 | bytes 17473540 | tf_op jit(solution)/shard_map/dot_general | solution.py:90
  76.4 28.3 %multiply_convert_fusion = f16[512,18992]{0,1:T(8,128)(2,1)} fusion(bf16[512,1024]{1,0:T(8,128)(2,1)S(1)} %bitcast.538, bf16[1024,18992]{0,1:T(8,128)(2,1)} %param.7), kind=kOutput, calls=%fused_computation | convolution fusion | flops 19934003200 | bytes 59392000 | tf_op jit(solution)/shard_map/dot_general | solution.py:50
  104.7 33.3 %reshape.409 = f16[4,128,18992]{1,0,2:T(4,128)(2,1)} reshape(f16[512,18992]{0,1:T(8,128)(2,1)} %multiply_convert_fusion) | data formatting | bytes 38895616 | tf_op jit(solution)/shard_map/reshape | solution.py:51
  138.0 57.0 %constant_dynamic-slice_fusion.21 = (f16[1,128,18992]{1,0,2:T(2,128)(2,1)}, f16[1,128,18992]{1,0,2:T(2,128)(2,1)}, f16[1,128,18992]{1,0,2:T(2,128)(2,1)}, f16[1,128,18992]{1,0,2:T(2,128)(2,1)}) fusion(f16[4,128,18992]{1,0,2:T(4,128)(2,1)} %reshape.409, s32[]{:T(128)S(6)} %select_n.225, s32[]{:T(128)S(6)} %select_n.227, s32[]{:T(128)S(6)} %select_n.226, ...), kind=kLoop, calls=%fused_computation.260 | loop fusion | bytes 38895632 | tf_op jit(solution)/shard_map/jit(dynamic_index_in_dim)/dynamic_slice | solution.py:40
  195.1 8.8 copy.208
  203.9 8.3 copy.209
  212.2 6.5 copy.207
  221.0 10.2 %abs_reduce_fusion.3 = (f32[256]{0:T(256)S(1)}, f32[256,9472]{1,0:T(8,128)}) fusion(f16[256,9472]{1,0:T(8,128)(2,1)} %collective-permute-done, bf16[640,37984]{0,1:T(8,128)(2,1)} %param.8, bf16[2,256,640]{2,1,0:T(8,128)(2,1)S(1)} %bitcast.543, s32[]{:T(128)S(6)} %select_n.217), kind=kOutput, calls=%fused_computation.32 | convolution fusion | flops 3115908864 | bytes 27001860 | tf_op jit(solution)/shard_map/dot_general | solution.py:91
  235.3 10.1 %abs_reduce_fusion.2 = (f32[256]{0:T(256)S(1)}, f32[256,9472]{1,0:T(8,128)}) fusion(f16[256,9472]{1,0:T(8,128)(2,1)} %collective-permute-done.18, bf16[640,37984]{0,1:T(8,128)(2,1)} %param.8, bf16[2,256,640]{2,1,0:T(8,128)(2,1)S(1)} %bitcast.544, s32[]{:T(128)S(6)} %select_n.217), kind=kOutput, calls=%fused_computation.30 | convolution fusion | flops 3115908864 | bytes 27001860 | tf_op jit(solution)/shard_map/dot_general | solution.py:91
  250.6 10.2 %abs_reduce_fusion.1 = (f32[256]{0:T(256)S(1)}, f32[256,9472]{1,0:T(8,128)}) fusion(f16[256,9472]{1,0:T(8,128)(2,1)} %collective-permute-done.25, bf16[640,37984]{0,1:T(8,128)(2,1)} %param.8, bf16[2,256,640]{2,1,0:T(8,128)(2,1)S(1)} %bitcast.545, s32[]{:T(128)S(6)} %select_n.217), kind=kOutput, calls=%fused_computation.28 | convolution fusion | flops 3115908864 | bytes 27001860 | tf_op jit(solution)/shard_map/dot_general | solution.py:91
  266.1 13.6 %abs_reduce_fusion = (f32[256]{0:T(256)S(1)}, f32[256,9568]{0,1:T(8,128)}) fusion(f16[256,9568]{0,1:T(8,128)(2,1)} %collective-permute-done.32, bf16[640,37984]{0,1:T(8,128)(2,1)} %param.8, bf16[2,256,640]{2,1,0:T(8,128)(2,1)S(1)} %bitcast.546, s32[]{:T(128)S(6)} %select_n.217), kind=kOutput, calls=%fused_computation.21 | convolution fusion | flops 3147489024 | bytes 27272196 | tf_op jit(solution)/shard_map/dot_general | solution.py:91
  279.8 11.2 %copy.152 = f32[256,9568]{1,0:T(8,128)} copy(f32[256,9568]{0,1:T(8,128)} %get-tuple-element.181) | data formatting | bytes 19595264 | tf_op jit(solution)/shard_map/add | solution.py:93
  310.3 17.5 %collective-permute-done.9 = f16[128,18992]{0,1:T(8,128)(2,1)} collective-permute-done((f16[128,18992]{0,1:T(8,128)(2,1)}, f16[128,18992]{0,1:T(8,128)(2,1)}, u32[]{:S(2)}, u32[]{:S(2)}) %collective-permute-start.9) | collective-permute-done | bytes 4861984 | tf_op jit(solution)/shard_map/ppermute | solution.py:55
  327.8 102.6 %collective-permute-done.7 = f16[128,18992]{0,1:T(8,128)(2,1)} collective-permute-done((f16[128,18992]{0,1:T(8,128)(2,1)}, f16[128,18992]{0,1:T(8,128)(2,1)}, u32[]{:S(2)}, u32[]{:S(2)}) %collective-permute-start.7) | collective-permute-done | bytes 4861984 | tf_op jit(solution)/shard_map/ppermute | solution.py:55
  431.0 11.5 %fusion.19 = bf16[128,18992]{0,1:T(8,128)(2,1)} fusion(f16[128,18992]{0,1:T(8,128)(2,1)} %collective-permute-done.9, f16[128,18992]{0,1:T(8,128)(2,1)} %collective-permute-done.8, f16[128,18992]{0,1:T(8,128)(2,1)} %collective-permute-done.7, f16[1,128,18992]{1,0,2:T(2,128)(2,1)} %get-tuple-element.105), kind=kLoop, calls=%fused_computation.27 | loop fusion | flops 21878784 | bytes 24309760 | tf_op jit(solution)/shard_map/convert_element_type | solution.py:56
  442.5 7.6 copy.139
  455.2 5.8 collective-permute-start.17
  470.0 12.5 %collective-permute-done.10 = bf16[16,18992]{1,0:T(8,128)(2,1)S(1)} collective-permute-done((bf16[16,18992]{1,0:T(8,128)(2,1)S(1)}, bf16[16,18992]{1,0:T(8,128)(2,1)S(1)}, u32[]{:S(2)}, u32[]{:S(2)}) %collective-permute-start.10) | collective-permute-done | bytes 607776 | tf_op jit(solution)/shard_map/ppermute | solution.py:75
  482.4 7.1 collective-permute-start.13
  489.6 25.5 %collective-permute-done.17 = bf16[16,18992]{1,0:T(8,128)(2,1)S(1)} collective-permute-done((bf16[16,18992]{1,0:T(8,128)(2,1)S(1)}, bf16[16,18992]{1,0:T(8,128)(2,1)S(1)}, u32[]{:S(2)}, u32[]{:S(2)}) %collective-permute-start.17) | collective-permute-done | bytes 607776 | tf_op jit(solution)/shard_map/ppermute | solution.py:75
  515.5 6.3 collective-permute-done.15
  523.0 20.6 %collective-permute-done.14 = bf16[16,18992]{1,0:T(8,128)(2,1)S(1)} collective-permute-done((bf16[16,18992]{1,0:T(8,128)(2,1)S(1)}, bf16[16,18992]{1,0:T(8,128)(2,1)S(1)}, u32[]{:S(2)}, u32[]{:S(2)}) %collective-permute-start.14) | collective-permute-done | bytes 607776 | tf_op jit(solution)/shard_map/ppermute | solution.py:75
  547.8 23.6 %collective-permute-done.11 = bf16[16,18992]{1,0:T(8,128)(2,1)S(1)} collective-permute-done((bf16[16,18992]{1,0:T(8,128)(2,1)S(1)}, bf16[16,18992]{1,0:T(8,128)(2,1)S(1)}, u32[]{:S(2)}, u32[]{:S(2)}) %collective-permute-start.11) | collective-permute-done | bytes 607776 | tf_op jit(solution)/shard_map/ppermute | solution.py:75
  574.5 7.8 fusion.181
  582.3 12.5 %collective-permute-done.2 = s16[64,9600]{1,0:T(8,128)(2,1)S(1)} collective-permute-done((s16[64,9600]{1,0:T(8,128)(2,1)S(1)}, s16[64,9600]{1,0:T(8,128)(2,1)S(1)}, u32[]{:S(2)}, u32[]{:S(2)}) %collective-permute-start.2) | collective-permute-done | bytes 1228832 | tf_op jit(solution)/shard_map/ppermute | solution.py:107
  596.0 25.2 %collective-permute-done.20 = s16[64,9600]{1,0:T(8,128)(2,1)} collective-permute-done((s16[64,9600]{1,0:T(8,128)(2,1)}, s16[64,9600]{1,0:T(8,128)(2,1)}, u32[]{:S(2)}, u32[]{:S(2)}) %collective-permute-start.20) | collective-permute-done | bytes 1228832 | tf_op jit(solution)/shard_map/ppermute | solution.py:107
  629.9 5.6 collective-permute-start.21
  640.4 7.2 collective-permute-done.27
  650.3 23.9 %collective-permute-done.34 = s16[64,9696]{1,0:T(8,128)(2,1)} collective-permute-done((s16[64,9696]{1,0:T(8,128)(2,1)S(1)}, s16[64,9696]{1,0:T(8,128)(2,1)}, u32[]{:S(2)}, u32[]{:S(2)}) %collective-permute-start.34) | collective-permute-done | bytes 1241120 | tf_op jit(solution)/shard_map/ppermute | solution.py:107
  687.7 5.6 collective-permute-start.28
  701.6 6.0 collective-permute-start.35
  709.8 17.1 %collective-permute-done.3 = s16[64,9600]{1,0:T(8,128)(2,1)} collective-permute-done((s16[64,9600]{1,0:T(8,128)(2,1)}, s16[64,9600]{1,0:T(8,128)(2,1)}, u32[]{:S(2)}, u32[]{:S(2)}) %collective-permute-start.3) | collective-permute-done | bytes 1228832 | tf_op jit(solution)/shard_map/ppermute | solution.py:107
  738.0 15.2 %collective-permute-done.28 = s16[64,9600]{1,0:T(8,128)(2,1)} collective-permute-done((s16[64,9600]{1,0:T(8,128)(2,1)}, s16[64,9600]{1,0:T(8,128)(2,1)}, u32[]{:S(2)}, u32[]{:S(2)}) %collective-permute-start.28) | collective-permute-done | bytes 1228832 | tf_op jit(solution)/shard_map/ppermute | solution.py:107
  761.9 18.0 %collective-permute-done.35 = s16[64,9696]{1,0:T(8,128)(2,1)} collective-permute-done((s16[64,9696]{1,0:T(8,128)(2,1)}, s16[64,9696]{1,0:T(8,128)(2,1)}, u32[]{:S(2)}, u32[]{:S(2)}) %collective-permute-start.35) | collective-permute-done | bytes 1241120 | tf_op jit(solution)/shard_map/ppermute | solution.py:107
  798.4 19.5 %collective-permute-done.30 = s16[64,9600]{1,0:T(8,128)(2,1)} collective-permute-done((s16[64,9600]{1,0:T(8,128)(2,1)}, s16[64,9600]{1,0:T(8,128)(2,1)}, u32[]{:S(2)}, u32[]{:S(2)}) %collective-permute-start.30) | collective-permute-done | bytes 1228832 | tf_op jit(solution)/shard_map/ppermute | solution.py:108
  824.7 19.8 %collective-permute-done.37 = s16[64,9696]{1,0:T(8,128)(2,1)S(1)} collective-permute-done((s16[64,9696]{1,0:T(8,128)(2,1)S(1)}, s16[64,9696]{1,0:T(8,128)(2,1)S(1)}, u32[]{:S(2)}, u32[]{:S(2)}) %collective-permute-start.37) | collective-permute-done | bytes 1241120 | tf_op jit(solution)/shard_map/ppermute | solution.py:108
  850.5 20.4 %collective-permute-done.24 = s16[64,9600]{1,0:T(8,128)(2,1)} collective-permute-done((s16[64,9600]{1,0:T(8,128)(2,1)}, s16[64,9600]{1,0:T(8,128)(2,1)}, u32[]{:S(2)}, u32[]{:S(2)}) %collective-permute-start.24) | collective-permute-done | bytes 1228832 | tf_op jit(solution)/shard_map/ppermute | solution.py:108
  871.8 25.4 %collective-permute-done.6 = s16[64,9600]{1,0:T(8,128)(2,1)} collective-permute-done((s16[64,9600]{1,0:T(8,128)(2,1)}, s16[64,9600]{1,0:T(8,128)(2,1)}, u32[]{:S(2)}, u32[]{:S(2)}) %collective-permute-start.6) | collective-permute-done | bytes 1228832 | tf_op jit(solution)/shard_map/ppermute | solution.py:108
  901.7 5.8 fusion.187
  907.6 16.0 %collective-permute-done.31 = s16[64,9600]{1,0:T(8,128)(2,1)} collective-permute-done((s16[64,9600]{1,0:T(8,128)(2,1)}, s16[64,9600]{1,0:T(8,128)(2,1)}, u32[]{:S(2)}, u32[]{:S(2)}) %collective-permute-start.31) | collective-permute-done | bytes 1228832 | tf_op jit(solution)/shard_map/ppermute | solution.py:108
  928.7 5.1 select_reduce_fusion.3
  933.9 15.5 %collective-permute-done.38 = s16[64,9696]{1,0:T(8,128)(2,1)} collective-permute-done((s16[64,9696]{1,0:T(8,128)(2,1)}, s16[64,9696]{1,0:T(8,128)(2,1)}, u32[]{:S(2)}, u32[]{:S(2)}) %collective-permute-start.38) | collective-permute-done | bytes 1241120 | tf_op jit(solution)/shard_map/ppermute | solution.py:108
  955.7 12.4 %all_gather.11 = f32[16,6,64]{2,1,0:T(8,128)S(1)} all-gather(f32[4,6,64]{2,1,0:T(8,128)S(1)} %pad_maximum_fusion.16), channel_id=1, replica_groups=mesh['tv'=8,'sv'=4] {'sv'}, dimensions={0}, use_global_device_ids=true | all-gather | bytes 30720 | tf_op jit(solution)/shard_map/all_gather | solution.py:141
  968.8 5.1 multiply_convert_fusion.4
  (278 shorter events, 177.8 us)
Async XLA Ops:
  7.2 67.9 %all-gather.2.cloned.1.call-start = ((), (), s32[]{:S(2)}) async-start(), calls=%async_computation | async-start | bytes 1179648 | tf_op jit(solution)/shard_map/all_gather | solution.py:46
  29.9 190.3 %collective-permute-start = (f16[256,9472]{1,0:T(8,128)(2,1)}, f16[256,9472]{1,0:T(8,128)(2,1)}, u32[]{:S(2)}, u32[]{:S(2)}) collective-permute-start(f16[256,9472]{1,0:T(8,128)(2,1)} %fusion.1), channel_id=1, source_target_pairs={{0,4},{4,0},{8,12},{12,8},{16,20},{20,16},{24,28},{28,24},{1,5},{5... | collective-permute-start | bytes 14549000 | tf_op jit(solution)/shard_map/ppermute | solution.py:92
  40.6 193.0 %collective-permute-start.18 = (f16[256,9472]{1,0:T(8,128)(2,1)}, f16[256,9472]{1,0:T(8,128)(2,1)}, u32[]{:S(2)}, u32[]{:S(2)}) collective-permute-start(f16[256,9472]{1,0:T(8,128)(2,1)} %fusion.2), channel_id=1, source_target_pairs={{0,4},{4,0},{8,12},{12,8},{16,20},{20,16},{24,28},{28,24},{1,5},{5... | collective-permute-start | bytes 14549000 | tf_op jit(solution)/shard_map/ppermute | solution.py:92
  51.7 197.2 %collective-permute-start.25 = (f16[256,9472]{1,0:T(8,128)(2,1)}, f16[256,9472]{1,0:T(8,128)(2,1)}, u32[]{:S(2)}, u32[]{:S(2)}) collective-permute-start(f16[256,9472]{1,0:T(8,128)(2,1)} %fusion.3), channel_id=1, source_target_pairs={{0,4},{4,0},{8,12},{12,8},{16,20},{20,16},{24,28},{28,24},{1,5},{5... | collective-permute-start | bytes 14549000 | tf_op jit(solution)/shard_map/ppermute | solution.py:92
  72.7 191.5 %collective-permute-start.32 = (f16[256,9568]{0,1:T(8,128)(2,1)}, f16[256,9568]{0,1:T(8,128)(2,1)}, u32[]{:S(2)}, u32[]{:S(2)}) collective-permute-start(f16[256,9568]{0,1:T(8,128)(2,1)} %fusion), channel_id=1, source_target_pairs={{0,4},{4,0},{8,12},{12,8},{16,20},{20,16},{24,28},{28,24},{1,5},{5... | collective-permute-start | bytes 14696456 | tf_op jit(solution)/shard_map/ppermute | solution.py:92
  195.0 17.2 %slice-start.3 = ((s8[9723904]{0:T(1024)(128)(4,1)}), s8[4194304]{0:T(1024)(128)(4,1)S(1)}, s32[]{:S(2)}) async-start(s8[9723904]{0:T(1024)(128)(4,1)} %bitcast.512), calls=%async_computation.4 | async-start | bytes 8388608
  195.1 17.2 %slice-start.4 = ((s8[9723904]{0:T(1024)(128)(4,1)}), s8[4194304]{0:T(1024)(128)(4,1)S(1)}, s32[]{:S(2)}) async-start(s8[9723904]{0:T(1024)(128)(4,1)} %bitcast.512), calls=%async_computation.5 | async-start | bytes 8388608
  218.8 109.0 %collective-permute-start.9 = (f16[128,18992]{0,1:T(8,128)(2,1)}, f16[128,18992]{0,1:T(8,128)(2,1)}, u32[]{:S(2)}, u32[]{:S(2)}) collective-permute-start(f16[128,18992]{0,1:T(8,128)(2,1)} %bitcast.501), channel_id=1, source_target_pairs={{0,3},{1,2},{2,1},{3,0},{4,7},{5,6},{6,5},{7,4},{8,11},{9,10},{10,... | collective-permute-start | bytes 14585864 | tf_op jit(solution)/shard_map/ppermute | solution.py:55
  220.3 210.1 %collective-permute-start.7 = (f16[128,18992]{0,1:T(8,128)(2,1)}, f16[128,18992]{0,1:T(8,128)(2,1)}, u32[]{:S(2)}, u32[]{:S(2)}) collective-permute-start(f16[128,18992]{0,1:T(8,128)(2,1)} %bitcast.503), channel_id=1, source_target_pairs={{0,1},{1,0},{2,3},{3,2},{4,5},{5,4},{6,7},{7,6},{8,9},{9,8},{10,11... | collective-permute-start | bytes 14585864 | tf_op jit(solution)/shard_map/ppermute | solution.py:55
  233.6 59.7 %collective-permute-start.1 = (s16[64,9600]{1,0:T(8,128)(2,1)S(1)}, s16[64,9600]{1,0:T(8,128)(2,1)}, u32[]{:S(2)}, u32[]{:S(2)}) collective-permute-start(s16[64,9600]{1,0:T(8,128)(2,1)S(1)} %fusion.28), channel_id=1, source_target_pairs={{0,8},{4,12},{1,9},{5,13},{2,10},{6,14},{3,11},{7,15}} | collective-permute-start | bytes 3686408 | tf_op jit(solution)/shard_map/ppermute | solution.py:107
  248.8 46.7 %collective-permute-start.19 = (s16[64,9600]{1,0:T(8,128)(2,1)}, s16[64,9600]{1,0:T(8,128)(2,1)}, u32[]{:S(2)}, u32[]{:S(2)}) collective-permute-start(s16[64,9600]{1,0:T(8,128)(2,1)} %fusion.34), channel_id=1, source_target_pairs={{0,8},{4,12},{1,9},{5,13},{2,10},{6,14},{3,11},{7,15}} | collective-permute-start | bytes 3686408 | tf_op jit(solution)/shard_map/ppermute | solution.py:107
  264.2 33.0 %collective-permute-start.26 = (s16[64,9600]{1,0:T(8,128)(2,1)}, s16[64,9600]{1,0:T(8,128)(2,1)}, u32[]{:S(2)}, u32[]{:S(2)}) collective-permute-start(s16[64,9600]{1,0:T(8,128)(2,1)} %fusion.40), channel_id=1, source_target_pairs={{0,8},{4,12},{1,9},{5,13},{2,10},{6,14},{3,11},{7,15}} | collective-permute-start | bytes 3686408 | tf_op jit(solution)/shard_map/ppermute | solution.py:107
  293.3 137.7 %collective-permute-start.8 = (f16[128,18992]{0,1:T(8,128)(2,1)}, f16[128,18992]{0,1:T(8,128)(2,1)}, u32[]{:S(2)}, u32[]{:S(2)}) collective-permute-start(f16[128,18992]{0,1:T(8,128)(2,1)} %bitcast.535), channel_id=1, source_target_pairs={{0,2},{1,3},{2,0},{3,1},{4,6},{5,7},{6,4},{7,5},{8,10},{9,11},{10,... | collective-permute-start | bytes 14585864 | tf_op jit(solution)/shard_map/ppermute | solution.py:55
  295.5 14.6 %collective-permute-start.33 = (s16[64,9696]{1,0:T(8,128)(2,1)S(1)}, s16[64,9696]{1,0:T(8,128)(2,1)S(1)}, u32[]{:S(2)}, u32[]{:S(2)}) collective-permute-start(s16[64,9696]{1,0:T(8,128)(2,1)S(1)} %fusion.20), channel_id=1, source_target_pairs={{0,8},{4,12},{1,9},{5,13},{2,10},{6,14},{3,11},{7,15}} | collective-permute-start | bytes 3723272 | tf_op jit(solution)/shard_map/ppermute | solution.py:107
  452.7 29.7 %collective-permute-start.10 = (bf16[16,18992]{1,0:T(8,128)(2,1)S(1)}, bf16[16,18992]{1,0:T(8,128)(2,1)S(1)}, u32[]{:S(2)}, u32[]{:S(2)}) collective-permute-start(bf16[16,18992]{1,0:T(8,128)(2,1)S(1)} %get-tuple-element.119), channel_id=1, source_target_pairs={{0,0},{1,8},{2,16},{3,24},{4,4},{5,12},{6,20},{7,28},{8,1},{9,9},{... | collective-permute-start | bytes 1823240 | tf_op jit(solution)/shard_map/ppermute | solution.py:75
  455.2 59.8 %collective-permute-start.17 = (bf16[16,18992]{1,0:T(8,128)(2,1)S(1)}, bf16[16,18992]{1,0:T(8,128)(2,1)S(1)}, u32[]{:S(2)}, u32[]{:S(2)}) collective-permute-start(bf16[16,18992]{1,0:T(8,128)(2,1)S(1)} %get-tuple-element.120), channel_id=1, source_target_pairs={{0,28},{1,4},{2,12},{3,20},{4,24},{5,0},{6,8},{7,16},{8,29},{9,5},... | collective-permute-start | bytes 1823240 | tf_op jit(solution)/shard_map/ppermute | solution.py:75
  461.0 54.0 %collective-permute-start.16 = (bf16[16,18992]{1,0:T(8,128)(2,1)S(1)}, bf16[16,18992]{1,0:T(8,128)(2,1)S(1)}, u32[]{:S(2)}, u32[]{:S(2)}) collective-permute-start(bf16[16,18992]{1,0:T(8,128)(2,1)S(1)} %get-tuple-element.121), channel_id=1, source_target_pairs={{0,20},{1,28},{2,4},{3,12},{4,16},{5,24},{6,0},{7,8},{8,21},{9,29}... | collective-permute-start | bytes 1823240 | tf_op jit(solution)/shard_map/ppermute | solution.py:75
  464.5 57.2 %copy-start.8 = (s16[64,9600]{1,0:T(8,128)(2,1)S(1)}, s16[64,9600]{1,0:T(8,128)(2,1)}, u32[]{:S(2)}) copy-start(s16[64,9600]{1,0:T(8,128)(2,1)} %fusion.29) | copy-start | bytes 3686404
  464.5 57.2 %collective-permute-start.15 = (bf16[16,18992]{1,0:T(8,128)(2,1)S(1)}, bf16[16,18992]{1,0:T(8,128)(2,1)S(1)}, u32[]{:S(2)}, u32[]{:S(2)}) collective-permute-start(bf16[16,18992]{1,0:T(8,128)(2,1)S(1)} %get-tuple-element.122), channel_id=1, source_target_pairs={{0,12},{1,20},{2,28},{3,4},{4,8},{5,16},{6,24},{7,0},{8,13},{9,21}... | collective-permute-start | bytes 1823240 | tf_op jit(solution)/shard_map/ppermute | solution.py:75
  466.0 77.7 %collective-permute-start.14 = (bf16[16,18992]{1,0:T(8,128)(2,1)S(1)}, bf16[16,18992]{1,0:T(8,128)(2,1)S(1)}, u32[]{:S(2)}, u32[]{:S(2)}) collective-permute-start(bf16[16,18992]{1,0:T(8,128)(2,1)S(1)} %get-tuple-element.123), channel_id=1, source_target_pairs={{0,4},{1,12},{2,20},{3,28},{4,0},{5,8},{6,16},{7,24},{8,5},{9,13},... | collective-permute-start | bytes 1823240 | tf_op jit(solution)/shard_map/ppermute | solution.py:75
  482.4 62.7 %collective-permute-start.13 = (bf16[16,18992]{1,0:T(8,128)(2,1)S(1)}, bf16[16,18992]{1,0:T(8,128)(2,1)S(1)}, u32[]{:S(2)}, u32[]{:S(2)}) collective-permute-start(bf16[16,18992]{1,0:T(8,128)(2,1)S(1)} %get-tuple-element.124), channel_id=1, source_target_pairs={{0,24},{1,0},{2,8},{3,16},{4,28},{5,4},{6,12},{7,20},{8,25},{9,1},... | collective-permute-start | bytes 1823240 | tf_op jit(solution)/shard_map/ppermute | solution.py:75
  515.1 31.4 %collective-permute-start.12 = (bf16[16,18992]{1,0:T(8,128)(2,1)S(1)}, bf16[16,18992]{1,0:T(8,128)(2,1)S(1)}, u32[]{:S(2)}, u32[]{:S(2)}) collective-permute-start(bf16[16,18992]{1,0:T(8,128)(2,1)S(1)} %get-tuple-element.125), channel_id=1, source_target_pairs={{0,16},{1,24},{2,0},{3,8},{4,20},{5,28},{6,4},{7,12},{8,17},{9,25}... | collective-permute-start | bytes 1823240 | tf_op jit(solution)/shard_map/ppermute | solution.py:75
  515.1 56.3 %collective-permute-start.11 = (bf16[16,18992]{1,0:T(8,128)(2,1)S(1)}, bf16[16,18992]{1,0:T(8,128)(2,1)S(1)}, u32[]{:S(2)}, u32[]{:S(2)}) collective-permute-start(bf16[16,18992]{1,0:T(8,128)(2,1)S(1)} %get-tuple-element.126), channel_id=1, source_target_pairs={{0,8},{1,16},{2,24},{3,0},{4,12},{5,20},{6,28},{7,4},{8,9},{9,17},... | collective-permute-start | bytes 1823240 | tf_op jit(solution)/shard_map/ppermute | solution.py:75
  521.7 73.1 %collective-permute-start.2 = (s16[64,9600]{1,0:T(8,128)(2,1)S(1)}, s16[64,9600]{1,0:T(8,128)(2,1)S(1)}, u32[]{:S(2)}, u32[]{:S(2)}) collective-permute-start(s16[64,9600]{1,0:T(8,128)(2,1)S(1)} %copy-done.8), channel_id=1, source_target_pairs={{0,8},{4,12},{8,16},{12,20},{1,9},{5,13},{9,17},{13,21},{2,10},{6,... | collective-permute-start | bytes 3686408 | tf_op jit(solution)/shard_map/ppermute | solution.py:107
  543.6 77.6 %collective-permute-start.20 = (s16[64,9600]{1,0:T(8,128)(2,1)}, s16[64,9600]{1,0:T(8,128)(2,1)}, u32[]{:S(2)}, u32[]{:S(2)}) collective-permute-start(s16[64,9600]{1,0:T(8,128)(2,1)} %fusion.35), channel_id=1, source_target_pairs={{0,8},{4,12},{8,16},{12,20},{1,9},{5,13},{9,17},{13,21},{2,10},{6,... | collective-permute-start | bytes 3686408 | tf_op jit(solution)/shard_map/ppermute | solution.py:107
  545.2 102.4 %collective-permute-start.27 = (s16[64,9600]{1,0:T(8,128)(2,1)}, s16[64,9600]{1,0:T(8,128)(2,1)}, u32[]{:S(2)}, u32[]{:S(2)}) collective-permute-start(s16[64,9600]{1,0:T(8,128)(2,1)} %fusion.41), channel_id=1, source_target_pairs={{0,8},{4,12},{8,16},{12,20},{1,9},{5,13},{9,17},{13,21},{2,10},{6,... | collective-permute-start | bytes 3686408 | tf_op jit(solution)/shard_map/ppermute | solution.py:107
  546.5 127.8 %collective-permute-start.34 = (s16[64,9696]{1,0:T(8,128)(2,1)S(1)}, s16[64,9696]{1,0:T(8,128)(2,1)}, u32[]{:S(2)}, u32[]{:S(2)}) collective-permute-start(s16[64,9696]{1,0:T(8,128)(2,1)S(1)} %fusion.21), channel_id=1, source_target_pairs={{0,8},{4,12},{8,16},{12,20},{1,9},{5,13},{9,17},{13,21},{2,10},{6,... | collective-permute-start | bytes 3723272 | tf_op jit(solution)/shard_map/ppermute | solution.py:107
  574.5 61.1 %slice-start.6 = ((s8[9699328]{0:T(1024)(128)(4,1)}), s8[1310720]{0:T(1024)(128)(4,1)S(1)}, s32[]{:S(2)}) async-start(s8[9699328]{0:T(1024)(128)(4,1)} %bitcast.519), calls=%async_computation.7 | async-start | bytes 2621440
  622.1 13.4 %slice-start.7 = ((s8[9699328]{0:T(1024)(128)(4,1)}), s8[4194304]{0:T(1024)(128)(4,1)S(1)}, s32[]{:S(2)}) async-start(s8[9699328]{0:T(1024)(128)(4,1)} %bitcast.519), calls=%async_computation.8 | async-start | bytes 8388608
  622.2 13.4 %slice-start.8 = ((s8[9699328]{0:T(1024)(128)(4,1)}), s8[4194304]{0:T(1024)(128)(4,1)S(1)}, s32[]{:S(2)}) async-start(s8[9699328]{0:T(1024)(128)(4,1)} %bitcast.519), calls=%async_computation.9 | async-start | bytes 8388608
  627.1 60.5 %collective-permute-start.22 = (s16[64,9600]{1,0:T(8,128)(2,1)}, s16[64,9600]{1,0:T(8,128)(2,1)}, u32[]{:S(2)}, u32[]{:S(2)}) collective-permute-start(s16[64,9600]{1,0:T(8,128)(2,1)} %fusion.37), channel_id=1, source_target_pairs={{28,20},{24,16},{29,21},{25,17},{30,22},{26,18},{31,23},{27,19}} | collective-permute-start | bytes 3686408 | tf_op jit(solution)/shard_map/ppermute | solution.py:108
  629.9 71.6 %collective-permute-start.21 = (s16[64,9600]{1,0:T(8,128)(2,1)}, s16[64,9600]{1,0:T(8,128)(2,1)}, u32[]{:S(2)}, u32[]{:S(2)}) collective-permute-start(s16[64,9600]{1,0:T(8,128)(2,1)} %fusion.36), channel_id=1, source_target_pairs={{0,8},{4,12},{8,16},{12,20},{16,24},{20,28},{1,9},{5,13},{9,17},{1... | collective-permute-start | bytes 3686408 | tf_op jit(solution)/shard_map/ppermute | solution.py:107
  636.3 46.6 %slice-start = ((s8[9830400]{0:T(1024)(128)(4,1)}), s8[1441792]{0:T(1024)(128)(4,1)S(1)}, s32[]{:S(2)}) async-start(s8[9830400]{0:T(1024)(128)(4,1)} %bitcast.509), calls=%async_computation.1 | async-start | bytes 2883584
  637.7 56.5 %collective-permute-start.4 = (s16[64,9600]{1,0:T(8,128)(2,1)}, s16[64,9600]{1,0:T(8,128)(2,1)}, u32[]{:S(2)}, u32[]{:S(2)}) collective-permute-start(s16[64,9600]{1,0:T(8,128)(2,1)} %fusion.31), channel_id=1, source_target_pairs={{28,20},{24,16},{29,21},{25,17},{30,22},{26,18},{31,23},{27,19}} | collective-permute-start | bytes 3686408 | tf_op jit(solution)/shard_map/ppermute | solution.py:108
  647.5 79.3 %collective-permute-start.3 = (s16[64,9600]{1,0:T(8,128)(2,1)}, s16[64,9600]{1,0:T(8,128)(2,1)}, u32[]{:S(2)}, u32[]{:S(2)}) collective-permute-start(s16[64,9600]{1,0:T(8,128)(2,1)} %fusion.30), channel_id=1, source_target_pairs={{0,8},{4,12},{8,16},{12,20},{16,24},{20,28},{1,9},{5,13},{9,17},{1... | collective-permute-start | bytes 3686408 | tf_op jit(solution)/shard_map/ppermute | solution.py:107
  680.2 51.0 %collective-permute-start.29 = (s16[64,9600]{1,0:T(8,128)(2,1)}, s16[64,9600]{1,0:T(8,128)(2,1)}, u32[]{:S(2)}, u32[]{:S(2)}) collective-permute-start(s16[64,9600]{1,0:T(8,128)(2,1)} %fusion.43), channel_id=1, source_target_pairs={{28,20},{24,16},{29,21},{25,17},{30,22},{26,18},{31,23},{27,19}} | collective-permute-start | bytes 3686408 | tf_op jit(solution)/shard_map/ppermute | solution.py:108
  687.7 65.6 %collective-permute-start.28 = (s16[64,9600]{1,0:T(8,128)(2,1)}, s16[64,9600]{1,0:T(8,128)(2,1)}, u32[]{:S(2)}, u32[]{:S(2)}) collective-permute-start(s16[64,9600]{1,0:T(8,128)(2,1)} %fusion.42), channel_id=1, source_target_pairs={{0,8},{4,12},{8,16},{12,20},{16,24},{20,28},{1,9},{5,13},{9,17},{1... | collective-permute-start | bytes 3686408 | tf_op jit(solution)/shard_map/ppermute | solution.py:107
  694.2 61.9 %collective-permute-start.36 = (s16[64,9696]{1,0:T(8,128)(2,1)}, s16[64,9696]{1,0:T(8,128)(2,1)}, u32[]{:S(2)}, u32[]{:S(2)}) collective-permute-start(s16[64,9696]{1,0:T(8,128)(2,1)} %fusion.23), channel_id=1, source_target_pairs={{28,20},{24,16},{29,21},{25,17},{30,22},{26,18},{31,23},{27,19}} | collective-permute-start | bytes 3723272 | tf_op jit(solution)/shard_map/ppermute | solution.py:108
  701.6 78.3 %collective-permute-start.35 = (s16[64,9696]{1,0:T(8,128)(2,1)}, s16[64,9696]{1,0:T(8,128)(2,1)}, u32[]{:S(2)}, u32[]{:S(2)}) collective-permute-start(s16[64,9696]{1,0:T(8,128)(2,1)} %fusion.22), channel_id=1, source_target_pairs={{0,8},{4,12},{8,16},{12,20},{16,24},{20,28},{1,9},{5,13},{9,17},{1... | collective-permute-start | bytes 3723272 | tf_op jit(solution)/shard_map/ppermute | solution.py:107
  726.9 53.9 %collective-permute-start.23 = (s16[64,9600]{1,0:T(8,128)(2,1)}, s16[64,9600]{1,0:T(8,128)(2,1)}, u32[]{:S(2)}, u32[]{:S(2)}) collective-permute-start(s16[64,9600]{1,0:T(8,128)(2,1)} %fusion.38), channel_id=1, source_target_pairs={{28,20},{24,16},{20,12},{16,8},{29,21},{25,17},{21,13},{17,9},{30,... | collective-permute-start | bytes 3686408 | tf_op jit(solution)/shard_map/ppermute | solution.py:108
  731.2 60.4 %collective-permute-start.5 = (s16[64,9600]{1,0:T(8,128)(2,1)}, s16[64,9600]{1,0:T(8,128)(2,1)}, u32[]{:S(2)}, u32[]{:S(2)}) collective-permute-start(s16[64,9600]{1,0:T(8,128)(2,1)} %fusion.32), channel_id=1, source_target_pairs={{28,20},{24,16},{20,12},{16,8},{29,21},{25,17},{21,13},{17,9},{30,... | collective-permute-start | bytes 3686408 | tf_op jit(solution)/shard_map/ppermute | solution.py:108
  753.2 64.7 %collective-permute-start.30 = (s16[64,9600]{1,0:T(8,128)(2,1)}, s16[64,9600]{1,0:T(8,128)(2,1)}, u32[]{:S(2)}, u32[]{:S(2)}) collective-permute-start(s16[64,9600]{1,0:T(8,128)(2,1)} %fusion.44), channel_id=1, source_target_pairs={{28,20},{24,16},{20,12},{16,8},{29,21},{25,17},{21,13},{17,9},{30,... | collective-permute-start | bytes 3686408 | tf_op jit(solution)/shard_map/ppermute | solution.py:108
  759.9 84.6 %collective-permute-start.37 = (s16[64,9696]{1,0:T(8,128)(2,1)S(1)}, s16[64,9696]{1,0:T(8,128)(2,1)S(1)}, u32[]{:S(2)}, u32[]{:S(2)}) collective-permute-start(s16[64,9696]{1,0:T(8,128)(2,1)S(1)} %fusion.24), channel_id=1, source_target_pairs={{28,20},{24,16},{20,12},{16,8},{29,21},{25,17},{21,13},{17,9},{30,... | collective-permute-start | bytes 3723272 | tf_op jit(solution)/shard_map/ppermute | solution.py:108
  785.7 85.2 %collective-permute-start.24 = (s16[64,9600]{1,0:T(8,128)(2,1)}, s16[64,9600]{1,0:T(8,128)(2,1)}, u32[]{:S(2)}, u32[]{:S(2)}) collective-permute-start(s16[64,9600]{1,0:T(8,128)(2,1)} %fusion.39), channel_id=1, source_target_pairs={{28,20},{24,16},{20,12},{16,8},{12,4},{8,0},{29,21},{25,17},{21,13... | collective-permute-start | bytes 3686408 | tf_op jit(solution)/shard_map/ppermute | solution.py:108
  796.5 100.8 %collective-permute-start.6 = (s16[64,9600]{1,0:T(8,128)(2,1)}, s16[64,9600]{1,0:T(8,128)(2,1)}, u32[]{:S(2)}, u32[]{:S(2)}) collective-permute-start(s16[64,9600]{1,0:T(8,128)(2,1)} %fusion.33), channel_id=1, source_target_pairs={{28,20},{24,16},{20,12},{16,8},{12,4},{8,0},{29,21},{25,17},{21,13... | collective-permute-start | bytes 3686408 | tf_op jit(solution)/shard_map/ppermute | solution.py:108
  822.8 100.8 %collective-permute-start.31 = (s16[64,9600]{1,0:T(8,128)(2,1)}, s16[64,9600]{1,0:T(8,128)(2,1)}, u32[]{:S(2)}, u32[]{:S(2)}) collective-permute-start(s16[64,9600]{1,0:T(8,128)(2,1)} %fusion.45), channel_id=1, source_target_pairs={{28,20},{24,16},{20,12},{16,8},{12,4},{8,0},{29,21},{25,17},{21,13... | collective-permute-start | bytes 3686408 | tf_op jit(solution)/shard_map/ppermute | solution.py:108
  848.4 100.9 %collective-permute-start.38 = (s16[64,9696]{1,0:T(8,128)(2,1)}, s16[64,9696]{1,0:T(8,128)(2,1)}, u32[]{:S(2)}, u32[]{:S(2)}) collective-permute-start(s16[64,9696]{1,0:T(8,128)(2,1)} %fusion.25), channel_id=1, source_target_pairs={{28,20},{24,16},{20,12},{16,8},{12,4},{8,0},{29,21},{25,17},{21,13... | collective-permute-start | bytes 3723272 | tf_op jit(solution)/shard_map/ppermute | solution.py:108
  901.7 26.5 %copy-start = (f32[64,9472]{1,0:T(8,128)}, f32[64,9472]{1,0:T(8,128)S(1)}, u32[]{:S(2)}) copy-start(f32[64,9472]{1,0:T(8,128)S(1)} %get-tuple-element.44) | copy-start | bytes 7274500
  (17 other events, 83.6 us)
Sparse Core Ops, SparseCore 0:
  9.6 27.8 all-gather.1

commit v2 on v1

--- a/solution.py
+++ b/solution.py
@@ -48,12 +48,13 @@
     rows = rows.reshape(tv_count, sv_count, share, rows.shape[1])
     rows = rows.transpose(1, 0, 2, 3).reshape(-1, rows.shape[-1])
     part = pack(jnp.dot(rows, teacher_head, preferred_element_type=jnp.float32))
-    part = part.reshape(sv_count, tv_count * share, part.shape[1])
-    total = unpack(block(part, here))
+    depth = tv_count * share
+    total = unpack(lax.dynamic_slice_in_dim(part, here * depth, depth))
     for flip in range(1, sv_count):
         swap = [(i, i ^ flip) for i in range(sv_count)]
-        total = total + unpack(lax.ppermute(block(part, here ^ flip), "sv", swap))
-    return total.astype(jnp.bfloat16).reshape(tv_count, share, part.shape[2])
+        given = lax.dynamic_slice_in_dim(part, (here ^ flip) * depth, depth)
+        total = total + unpack(lax.ppermute(given, "sv", swap))
+    return total.astype(jnp.bfloat16).reshape(tv_count, share, part.shape[1])
 
 
 def place_teacher(logit):

time: 992 us -> 966 us (0.974)
  local copies, waits for them, and re-layouts: 154 us -> 52 us
  waiting for transfers between devices: 450 us -> 531 us
    ppermute x3, waiting for transfers between devices: 121 us -> 194 us  [reduce_teacher(): total = total + unpack(lax.ppermute(given, 'sv', swap))]
    dynamic_slice x1, local copies, waits for them, and re-layouts: 57 us -> 12.5 us  [reduce_teacher(): given = lax.dynamic_slice_in_dim(part, (here ^ flip) * depth, depth)]
    reshape x1 -> x0, local copies, waits for them, and re-layouts: 33.3 us -> none  [reduce_teacher(): part = part.reshape(sv_count, tv_count * share, part.shape[1])]
    unnamed x77 -> x68, local copies, waits for them, and re-layouts: 27.2 us -> 3.47 us
  transfers between devices with their start and end apart: 40 -> 40, of which waited for: 22 -> 22; matrix products, arithmetic and copies ran while one was open for 39% -> 29% of each run, Pallas kernels for 0% -> 0%
where the time goes in v2:
time: 966 us; the launch traced here: 954 us
  waiting for transfers between devices  531 us (55%)
  other arithmetic  138 us (14%)
  matrix products  126 us (13%)
  starting transfers between devices  73.2 us (8%)
  local copies, waits for them, and re-layouts  52 us (5%)
  blocking collectives  19.5 us (2%)
  between operations  15.1 us (2%)
    ppermute x3, waiting for transfers between devices, reduce_teacher(): total = total + unpack(lax.ppermute(given, 'sv', swap))  194 us
    ppermute x12, waiting for transfers between devices, reduce_student(): up = lax.ppermute(quantize(send_up, limit_up), 'tv', up_pairs)  122 us
    ppermute x12, waiting for transfers between devices, reduce_student(): down = lax.ppermute(quantize(send_down, limit_down), 'tv', down_pairs)  121 us
    ppermute x8, waiting for transfers between devices, place_teacher(): row.append(lax.ppermute(mine, ('tv', 'sv'), pairs))  94.3 us
    dot_general x4, matrix products, reduce_student(): given = pack(jnp.dot(rows[1], head, preferred_element_type=jnp.float32))  52.7 us
    mul x38, other arithmetic, quantize(): scaled = values * (TOP * jnp.exp2(code * (-1.0 / STEPS)))  48.3 us
    dot_general x4, matrix products, reduce_student(): kept = jnp.dot(rows[0], head, preferred_element_type=jnp.float32)  44.6 us
    ppermute x12, starting transfers between devices, reduce_student(): up = lax.ppermute(quantize(send_up, limit_up), 'tv', up_pairs)  30 us
  transfers between devices with their start and end apart: 40, of which 22 were waited for; matrix products, arithmetic and copies ran while one was open for 29% of the time, Pallas kernels for 0%

profile of v2, /device:TPU:16, one launch (start us, length us, event | category | flops | bytes accessed | tf_op | source)
XLA Modules:
  0.0 954.3 jit_solution(12625725698432983127)
XLA Ops:
  7.9 11.3 %all_gather.9 = bf16[512,640]{1,0:T(8,128)(2,1)S(1)} all-gather(bf16[128,640]{1,0:T(8,128)(2,1)} %param.6), channel_id=1, replica_groups=mesh['tv'=8,'sv'=4] {'sv'}, dimensions={0}, use_global_device_ids=true | all-gather | bytes 819200 | tf_op jit(solution)/shard_map/all_gather | solution.py:130
  19.3 10.7 %fusion.1 = f16[256,9472]{1,0:T(8,128)(2,1)} fusion(bf16[640,37984]{0,1:T(8,128)(2,1)} %param.8, bf16[2,256,640]{2,1,0:T(8,128)(2,1)S(1)} %bitcast.520, s32[]{:T(128)S(6)} %select_n.217), kind=kOutput, calls=%fused_computation.6 | convolution fusion | flops 3108634624 | bytes 17301508 | tf_op jit(solution)/shard_map/dot_general | solution.py:91
  30.0 10.6 %fusion.2 = f16[256,9472]{1,0:T(8,128)(2,1)} fusion(bf16[640,37984]{0,1:T(8,128)(2,1)} %param.8, bf16[2,256,640]{2,1,0:T(8,128)(2,1)S(1)} %bitcast.521, s32[]{:T(128)S(6)} %select_n.217), kind=kOutput, calls=%fused_computation.7 | convolution fusion | flops 3108634624 | bytes 17301508 | tf_op jit(solution)/shard_map/dot_general | solution.py:91
  41.1 10.7 %fusion.3 = f16[256,9472]{1,0:T(8,128)(2,1)} fusion(bf16[640,37984]{0,1:T(8,128)(2,1)} %param.8, bf16[2,256,640]{2,1,0:T(8,128)(2,1)S(1)} %bitcast.522, s32[]{:T(128)S(6)} %select_n.217), kind=kOutput, calls=%fused_computation.8 | convolution fusion | flops 3108634624 | bytes 17301508 | tf_op jit(solution)/shard_map/dot_general | solution.py:91
  51.8 20.7 %fusion = f16[256,9568]{0,1:T(8,128)(2,1)} fusion(bf16[640,37984]{0,1:T(8,128)(2,1)} %param.8, bf16[2,256,640]{2,1,0:T(8,128)(2,1)S(1)} %bitcast.523, s32[]{:T(128)S(6)} %select_n.217), kind=kOutput, calls=%fused_computation.5 | convolution fusion | flops 3140141056 | bytes 17473540 | tf_op jit(solution)/shard_map/dot_general | solution.py:91
  76.2 28.3 %multiply_convert_fusion = f16[512,18992]{0,1:T(8,128)(2,1)} fusion(bf16[512,1024]{1,0:T(8,128)(2,1)S(1)} %bitcast.519, bf16[1024,18992]{0,1:T(8,128)(2,1)} %param.7), kind=kOutput, calls=%fused_computation | convolution fusion | flops 19934003200 | bytes 59392000 | tf_op jit(solution)/shard_map/dot_general | solution.py:50
  104.5 12.5 %constant_dynamic-slice_fusion.20 = (f16[128,18992]{0,1:T(8,128)(2,1)}, f16[128,18992]{0,1:T(8,128)(2,1)}, f16[128,18992]{0,1:T(8,128)(2,1)}) fusion(f16[512,18992]{0,1:T(8,128)(2,1)} %multiply_convert_fusion, s32[]{:T(128)S(6)} %select_n.225, s32[]{:T(128)S(6)} %select_n.227, s32[]{:T(128)S(6)} %select_n.226), kind=kLoop, calls=%fused_computation.251 | loop fusion | bytes 29171724 | tf_op jit(solution)/shard_map/dynamic_slice | solution.py:55
  119.1 10.2 %abs_reduce_fusion.3 = (f32[256]{0:T(256)S(1)}, f32[256,9472]{1,0:T(8,128)}) fusion(f16[256,9472]{1,0:T(8,128)(2,1)} %collective-permute-done, bf16[640,37984]{0,1:T(8,128)(2,1)} %param.8, bf16[2,256,640]{2,1,0:T(8,128)(2,1)S(1)} %bitcast.524, s32[]{:T(128)S(6)} %select_n.216), kind=kOutput, calls=%fused_computation.28 | convolution fusion | flops 3115908864 | bytes 27001860 | tf_op jit(solution)/shard_map/dot_general | solution.py:92
  133.5 10.6 %abs_reduce_fusion.2 = (f32[256]{0:T(256)S(1)}, f32[256,9472]{1,0:T(8,128)}) fusion(f16[256,9472]{1,0:T(8,128)(2,1)} %collective-permute-done.18, bf16[640,37984]{0,1:T(8,128)(2,1)} %param.8, bf16[2,256,640]{2,1,0:T(8,128)(2,1)S(1)} %bitcast.525, s32[]{:T(128)S(6)} %select_n.216), kind=kOutput, calls=%fused_computation.26 | convolution fusion | flops 3115908864 | bytes 27001860 | tf_op jit(solution)/shard_map/dot_general | solution.py:92
  149.2 10.2 %abs_reduce_fusion.1 = (f32[256]{0:T(256)S(1)}, f32[256,9472]{1,0:T(8,128)}) fusion(f16[256,9472]{1,0:T(8,128)(2,1)} %collective-permute-done.25, bf16[640,37984]{0,1:T(8,128)(2,1)} %param.8, bf16[2,256,640]{2,1,0:T(8,128)(2,1)S(1)} %bitcast.526, s32[]{:T(128)S(6)} %select_n.216), kind=kOutput, calls=%fused_computation.24 | convolution fusion | flops 3115908864 | bytes 27001860 | tf_op jit(solution)/shard_map/dot_general | solution.py:92
  164.5 13.6 %abs_reduce_fusion = (f32[256]{0:T(256)S(1)}, f32[256,9568]{0,1:T(8,128)}) fusion(f16[256,9568]{0,1:T(8,128)(2,1)} %collective-permute-done.32, bf16[640,37984]{0,1:T(8,128)(2,1)} %param.8, bf16[2,256,640]{2,1,0:T(8,128)(2,1)S(1)} %bitcast.527, s32[]{:T(128)S(6)} %select_n.216), kind=kOutput, calls=%fused_computation.21 | convolution fusion | flops 3147489024 | bytes 27272196 | tf_op jit(solution)/shard_map/dot_general | solution.py:92
  178.3 11.1 %copy.140 = f32[256,9568]{1,0:T(8,128)} copy(f32[256,9568]{0,1:T(8,128)} %get-tuple-element.180) | data formatting | bytes 19595264 | tf_op jit(solution)/shard_map/add | solution.py:94
  209.0 15.9 %collective-permute-done.7 = f16[128,18992]{0,1:T(8,128)(2,1)} collective-permute-done((f16[128,18992]{0,1:T(8,128)(2,1)}, f16[128,18992]{0,1:T(8,128)(2,1)}, u32[]{:S(2)}, u32[]{:S(2)}) %collective-permute-start.7) | collective-permute-done | bytes 4861984 | tf_op jit(solution)/shard_map/ppermute | solution.py:56
  225.0 103.5 %collective-permute-done.9 = f16[128,18992]{0,1:T(8,128)(2,1)} collective-permute-done((f16[128,18992]{0,1:T(8,128)(2,1)}, f16[128,18992]{0,1:T(8,128)(2,1)}, u32[]{:S(2)}, u32[]{:S(2)}) %collective-permute-start.9) | collective-permute-done | bytes 4861984 | tf_op jit(solution)/shard_map/ppermute | solution.py:56
  328.5 74.0 %collective-permute-done.8 = f16[128,18992]{0,1:T(8,128)(2,1)} collective-permute-done((f16[128,18992]{0,1:T(8,128)(2,1)}, f16[128,18992]{0,1:T(8,128)(2,1)}, u32[]{:S(2)}, u32[]{:S(2)}) %collective-permute-start.8) | collective-permute-done | bytes 4861984 | tf_op jit(solution)/shard_map/ppermute | solution.py:56
  402.6 10.2 %multiply_convert_fusion.1 = bf16[128,18992]{0,1:T(8,128)(2,1)} fusion(f16[128,18992]{0,1:T(8,128)(2,1)} %collective-permute-done.9, f16[128,18992]{0,1:T(8,128)(2,1)} %collective-permute-done.8, f16[128,18992]{0,1:T(8,128)(2,1)} %collective-permute-done.7, f16[512,18992]{0,1:T(8,128)(2,1)} %multiply_convert_fusion, s32[]{:T(128)S(6)} %select_n.224), kind=kLoop, calls=%fused_computation.23 | loop fusion | flops 21878784 | bytes 24309764 | tf_op jit(solution)/shard_map/convert_element_type | solution.py:57
  412.8 7.6 copy.127
  423.1 6.7 collective-permute-start.10
  429.8 4.1 collective-permute-start.17
  438.9 4.0 collective-permute-start.14
  442.9 41.7 %collective-permute-done.10 = bf16[16,18992]{1,0:T(8,128)(2,1)S(1)} collective-permute-done((bf16[16,18992]{1,0:T(8,128)(2,1)S(1)}, bf16[16,18992]{1,0:T(8,128)(2,1)S(1)}, u32[]{:S(2)}, u32[]{:S(2)}) %collective-permute-start.10) | collective-permute-done | bytes 607776 | tf_op jit(solution)/shard_map/ppermute | solution.py:76
  484.5 5.5 collective-permute-done.17
  490.4 7.4 collective-permute-done.15
  499.1 31.8 %collective-permute-done.14 = bf16[16,18992]{1,0:T(8,128)(2,1)S(1)} collective-permute-done((bf16[16,18992]{1,0:T(8,128)(2,1)S(1)}, bf16[16,18992]{1,0:T(8,128)(2,1)S(1)}, u32[]{:S(2)}, u32[]{:S(2)}) %collective-permute-start.14) | collective-permute-done | bytes 607776 | tf_op jit(solution)/shard_map/ppermute | solution.py:76
  534.8 7.9 collective-permute-done.11
  545.8 7.7 fusion.177
  553.6 15.1 %collective-permute-done.2 = s16[64,9600]{1,0:T(8,128)(2,1)S(1)} collective-permute-done((s16[64,9600]{1,0:T(8,128)(2,1)S(1)}, s16[64,9600]{1,0:T(8,128)(2,1)S(1)}, u32[]{:S(2)}, u32[]{:S(2)}) %collective-permute-start.2) | collective-permute-done | bytes 1228832 | tf_op jit(solution)/shard_map/ppermute | solution.py:108
  569.9 25.2 %collective-permute-done.20 = s16[64,9600]{1,0:T(8,128)(2,1)} collective-permute-done((s16[64,9600]{1,0:T(8,128)(2,1)}, s16[64,9600]{1,0:T(8,128)(2,1)}, u32[]{:S(2)}, u32[]{:S(2)}) %collective-permute-start.20) | collective-permute-done | bytes 1228832 | tf_op jit(solution)/shard_map/ppermute | solution.py:108
  604.3 5.6 collective-permute-start.21
  614.7 6.7 collective-permute-done.27
  624.3 23.9 %collective-permute-done.34 = s16[64,9696]{1,0:T(8,128)(2,1)} collective-permute-done((s16[64,9696]{1,0:T(8,128)(2,1)S(1)}, s16[64,9696]{1,0:T(8,128)(2,1)}, u32[]{:S(2)}, u32[]{:S(2)}) %collective-permute-start.34) | collective-permute-done | bytes 1241120 | tf_op jit(solution)/shard_map/ppermute | solution.py:108
  661.6 5.6 collective-permute-start.28
  675.5 5.6 collective-permute-start.35
  683.5 17.4 %collective-permute-done.3 = s16[64,9600]{1,0:T(8,128)(2,1)} collective-permute-done((s16[64,9600]{1,0:T(8,128)(2,1)}, s16[64,9600]{1,0:T(8,128)(2,1)}, u32[]{:S(2)}, u32[]{:S(2)}) %collective-permute-start.3) | collective-permute-done | bytes 1228832 | tf_op jit(solution)/shard_map/ppermute | solution.py:108
  712.0 15.2 %collective-permute-done.28 = s16[64,9600]{1,0:T(8,128)(2,1)} collective-permute-done((s16[64,9600]{1,0:T(8,128)(2,1)}, s16[64,9600]{1,0:T(8,128)(2,1)}, u32[]{:S(2)}, u32[]{:S(2)}) %collective-permute-start.28) | collective-permute-done | bytes 1228832 | tf_op jit(solution)/shard_map/ppermute | solution.py:108
  735.8 18.0 %collective-permute-done.35 = s16[64,9696]{1,0:T(8,128)(2,1)} collective-permute-done((s16[64,9696]{1,0:T(8,128)(2,1)}, s16[64,9696]{1,0:T(8,128)(2,1)}, u32[]{:S(2)}, u32[]{:S(2)}) %collective-permute-start.35) | collective-permute-done | bytes 1241120 | tf_op jit(solution)/shard_map/ppermute | solution.py:108
  761.7 3.8 collective-permute-done.5
  772.5 19.3 %collective-permute-done.30 = s16[64,9600]{1,0:T(8,128)(2,1)} collective-permute-done((s16[64,9600]{1,0:T(8,128)(2,1)}, s16[64,9600]{1,0:T(8,128)(2,1)}, u32[]{:S(2)}, u32[]{:S(2)}) %collective-permute-start.30) | collective-permute-done | bytes 1228832 | tf_op jit(solution)/shard_map/ppermute | solution.py:109
  798.7 19.7 %collective-permute-done.37 = s16[64,9696]{1,0:T(8,128)(2,1)S(1)} collective-permute-done((s16[64,9696]{1,0:T(8,128)(2,1)S(1)}, s16[64,9696]{1,0:T(8,128)(2,1)S(1)}, u32[]{:S(2)}, u32[]{:S(2)}) %collective-permute-start.37) | collective-permute-done | bytes 1241120 | tf_op jit(solution)/shard_map/ppermute | solution.py:109
  824.2 20.6 %collective-permute-done.24 = s16[64,9600]{1,0:T(8,128)(2,1)} collective-permute-done((s16[64,9600]{1,0:T(8,128)(2,1)}, s16[64,9600]{1,0:T(8,128)(2,1)}, u32[]{:S(2)}, u32[]{:S(2)}) %collective-permute-start.24) | collective-permute-done | bytes 1228832 | tf_op jit(solution)/shard_map/ppermute | solution.py:109
  845.7 25.4 %collective-permute-done.6 = s16[64,9600]{1,0:T(8,128)(2,1)} collective-permute-done((s16[64,9600]{1,0:T(8,128)(2,1)}, s16[64,9600]{1,0:T(8,128)(2,1)}, u32[]{:S(2)}, u32[]{:S(2)}) %collective-permute-start.6) | collective-permute-done | bytes 1228832 | tf_op jit(solution)/shard_map/ppermute | solution.py:109
  875.7 5.8 fusion.183
  881.5 16.0 %collective-permute-done.31 = s16[64,9600]{1,0:T(8,128)(2,1)} collective-permute-done((s16[64,9600]{1,0:T(8,128)(2,1)}, s16[64,9600]{1,0:T(8,128)(2,1)}, u32[]{:S(2)}, u32[]{:S(2)}) %collective-permute-start.31) | collective-permute-done | bytes 1228832 | tf_op jit(solution)/shard_map/ppermute | solution.py:109
  898.5 3.7 fusion.185
  902.6 5.1 select_reduce_fusion.3
  907.8 15.5 %collective-permute-done.38 = s16[64,9696]{1,0:T(8,128)(2,1)} collective-permute-done((s16[64,9696]{1,0:T(8,128)(2,1)}, s16[64,9696]{1,0:T(8,128)(2,1)}, u32[]{:S(2)}, u32[]{:S(2)}) %collective-permute-start.38) | collective-permute-done | bytes 1241120 | tf_op jit(solution)/shard_map/ppermute | solution.py:109
  929.6 8.2 all_gather.11
  938.5 5.2 multiply_convert_fusion.5
  (267 shorter events, 163.7 us)
Async XLA Ops:
  7.2 67.7 %all-gather.2.cloned.1.call-start = ((), (), s32[]{:S(2)}) async-start(), calls=%async_computation | async-start | bytes 1179648 | tf_op jit(solution)/shard_map/all_gather | solution.py:46
  30.0 87.7 %collective-permute-start = (f16[256,9472]{1,0:T(8,128)(2,1)}, f16[256,9472]{1,0:T(8,128)(2,1)}, u32[]{:S(2)}, u32[]{:S(2)}) collective-permute-start(f16[256,9472]{1,0:T(8,128)(2,1)} %fusion.1), channel_id=1, source_target_pairs={{0,4},{4,0},{8,12},{12,8},{16,20},{20,16},{24,28},{28,24},{1,5},{5... | collective-permute-start | bytes 14549000 | tf_op jit(solution)/shard_map/ppermute | solution.py:93
  40.6 91.1 %collective-permute-start.18 = (f16[256,9472]{1,0:T(8,128)(2,1)}, f16[256,9472]{1,0:T(8,128)(2,1)}, u32[]{:S(2)}, u32[]{:S(2)}) collective-permute-start(f16[256,9472]{1,0:T(8,128)(2,1)} %fusion.2), channel_id=1, source_target_pairs={{0,4},{4,0},{8,12},{12,8},{16,20},{20,16},{24,28},{28,24},{1,5},{5... | collective-permute-start | bytes 14549000 | tf_op jit(solution)/shard_map/ppermute | solution.py:93
  51.8 95.7 %collective-permute-start.25 = (f16[256,9472]{1,0:T(8,128)(2,1)}, f16[256,9472]{1,0:T(8,128)(2,1)}, u32[]{:S(2)}, u32[]{:S(2)}) collective-permute-start(f16[256,9472]{1,0:T(8,128)(2,1)} %fusion.3), channel_id=1, source_target_pairs={{0,4},{4,0},{8,12},{12,8},{16,20},{20,16},{24,28},{28,24},{1,5},{5... | collective-permute-start | bytes 14549000 | tf_op jit(solution)/shard_map/ppermute | solution.py:93
  72.5 90.3 %collective-permute-start.32 = (f16[256,9568]{0,1:T(8,128)(2,1)}, f16[256,9568]{0,1:T(8,128)(2,1)}, u32[]{:S(2)}, u32[]{:S(2)}) collective-permute-start(f16[256,9568]{0,1:T(8,128)(2,1)} %fusion), channel_id=1, source_target_pairs={{0,4},{4,0},{8,12},{12,8},{16,20},{20,16},{24,28},{28,24},{1,5},{5... | collective-permute-start | bytes 14696456 | tf_op jit(solution)/shard_map/ppermute | solution.py:93
  116.9 108.1 %collective-permute-start.7 = (f16[128,18992]{0,1:T(8,128)(2,1)}, f16[128,18992]{0,1:T(8,128)(2,1)}, u32[]{:S(2)}, u32[]{:S(2)}) collective-permute-start(f16[128,18992]{0,1:T(8,128)(2,1)} %get-tuple-element.105), channel_id=1, source_target_pairs={{0,1},{1,0},{2,3},{3,2},{4,5},{5,4},{6,7},{7,6},{8,9},{9,8},{10,11... | collective-permute-start | bytes 14585864 | tf_op jit(solution)/shard_map/ppermute | solution.py:56
  117.7 210.9 %collective-permute-start.9 = (f16[128,18992]{0,1:T(8,128)(2,1)}, f16[128,18992]{0,1:T(8,128)(2,1)}, u32[]{:S(2)}, u32[]{:S(2)}) collective-permute-start(f16[128,18992]{0,1:T(8,128)(2,1)} %get-tuple-element.106), channel_id=1, source_target_pairs={{0,3},{1,2},{2,1},{3,0},{4,7},{5,6},{6,5},{7,4},{8,11},{9,10},{10,... | collective-permute-start | bytes 14585864 | tf_op jit(solution)/shard_map/ppermute | solution.py:56
  131.7 60.0 %collective-permute-start.1 = (s16[64,9600]{1,0:T(8,128)(2,1)S(1)}, s16[64,9600]{1,0:T(8,128)(2,1)}, u32[]{:S(2)}, u32[]{:S(2)}) collective-permute-start(s16[64,9600]{1,0:T(8,128)(2,1)S(1)} %fusion.24), channel_id=1, source_target_pairs={{0,8},{4,12},{1,9},{5,13},{2,10},{6,14},{3,11},{7,15}} | collective-permute-start | bytes 3686408 | tf_op jit(solution)/shard_map/ppermute | solution.py:108
  147.5 46.5 %collective-permute-start.19 = (s16[64,9600]{1,0:T(8,128)(2,1)}, s16[64,9600]{1,0:T(8,128)(2,1)}, u32[]{:S(2)}, u32[]{:S(2)}) collective-permute-start(s16[64,9600]{1,0:T(8,128)(2,1)} %fusion.30), channel_id=1, source_target_pairs={{0,8},{4,12},{1,9},{5,13},{2,10},{6,14},{3,11},{7,15}} | collective-permute-start | bytes 3686408 | tf_op jit(solution)/shard_map/ppermute | solution.py:108
  162.8 33.1 %collective-permute-start.26 = (s16[64,9600]{1,0:T(8,128)(2,1)}, s16[64,9600]{1,0:T(8,128)(2,1)}, u32[]{:S(2)}, u32[]{:S(2)}) collective-permute-start(s16[64,9600]{1,0:T(8,128)(2,1)} %fusion.36), channel_id=1, source_target_pairs={{0,8},{4,12},{1,9},{5,13},{2,10},{6,14},{3,11},{7,15}} | collective-permute-start | bytes 3686408 | tf_op jit(solution)/shard_map/ppermute | solution.py:108
  191.7 210.8 %collective-permute-start.8 = (f16[128,18992]{0,1:T(8,128)(2,1)}, f16[128,18992]{0,1:T(8,128)(2,1)}, u32[]{:S(2)}, u32[]{:S(2)}) collective-permute-start(f16[128,18992]{0,1:T(8,128)(2,1)} %get-tuple-element.107), channel_id=1, source_target_pairs={{0,2},{1,3},{2,0},{3,1},{4,6},{5,7},{6,4},{7,5},{8,10},{9,11},{10,... | collective-permute-start | bytes 14585864 | tf_op jit(solution)/shard_map/ppermute | solution.py:56
  194.0 14.9 %collective-permute-start.33 = (s16[64,9696]{1,0:T(8,128)(2,1)S(1)}, s16[64,9696]{1,0:T(8,128)(2,1)S(1)}, u32[]{:S(2)}, u32[]{:S(2)}) collective-permute-start(s16[64,9696]{1,0:T(8,128)(2,1)S(1)} %fusion.16), channel_id=1, source_target_pairs={{0,8},{4,12},{1,9},{5,13},{2,10},{6,14},{3,11},{7,15}} | collective-permute-start | bytes 3723272 | tf_op jit(solution)/shard_map/ppermute | solution.py:108
  423.1 61.5 %collective-permute-start.10 = (bf16[16,18992]{1,0:T(8,128)(2,1)S(1)}, bf16[16,18992]{1,0:T(8,128)(2,1)S(1)}, u32[]{:S(2)}, u32[]{:S(2)}) collective-permute-start(bf16[16,18992]{1,0:T(8,128)(2,1)S(1)} %get-tuple-element.118), channel_id=1, source_target_pairs={{0,0},{1,8},{2,16},{3,24},{4,4},{5,12},{6,20},{7,28},{8,1},{9,9},{... | collective-permute-start | bytes 1823240 | tf_op jit(solution)/shard_map/ppermute | solution.py:76
  429.8 60.2 %collective-permute-start.17 = (bf16[16,18992]{1,0:T(8,128)(2,1)S(1)}, bf16[16,18992]{1,0:T(8,128)(2,1)S(1)}, u32[]{:S(2)}, u32[]{:S(2)}) collective-permute-start(bf16[16,18992]{1,0:T(8,128)(2,1)S(1)} %get-tuple-element.119), channel_id=1, source_target_pairs={{0,28},{1,4},{2,12},{3,20},{4,24},{5,0},{6,8},{7,16},{8,29},{9,5},... | collective-permute-start | bytes 1823240 | tf_op jit(solution)/shard_map/ppermute | solution.py:76
  433.9 56.1 %collective-permute-start.16 = (bf16[16,18992]{1,0:T(8,128)(2,1)S(1)}, bf16[16,18992]{1,0:T(8,128)(2,1)S(1)}, u32[]{:S(2)}, u32[]{:S(2)}) collective-permute-start(bf16[16,18992]{1,0:T(8,128)(2,1)S(1)} %get-tuple-element.120), channel_id=1, source_target_pairs={{0,20},{1,28},{2,4},{3,12},{4,16},{5,24},{6,0},{7,8},{8,21},{9,29}... | collective-permute-start | bytes 1823240 | tf_op jit(solution)/shard_map/ppermute | solution.py:76
  437.4 60.4 %copy-start.8 = (s16[64,9600]{1,0:T(8,128)(2,1)S(1)}, s16[64,9600]{1,0:T(8,128)(2,1)}, u32[]{:S(2)}) copy-start(s16[64,9600]{1,0:T(8,128)(2,1)} %fusion.25) | copy-start | bytes 3686404
  437.4 60.4 %collective-permute-start.15 = (bf16[16,18992]{1,0:T(8,128)(2,1)S(1)}, bf16[16,18992]{1,0:T(8,128)(2,1)S(1)}, u32[]{:S(2)}, u32[]{:S(2)}) collective-permute-start(bf16[16,18992]{1,0:T(8,128)(2,1)S(1)} %get-tuple-element.121), channel_id=1, source_target_pairs={{0,12},{1,20},{2,28},{3,4},{4,8},{5,16},{6,24},{7,0},{8,13},{9,21}... | collective-permute-start | bytes 1823240 | tf_op jit(solution)/shard_map/ppermute | solution.py:76
  438.9 92.0 %collective-permute-start.14 = (bf16[16,18992]{1,0:T(8,128)(2,1)S(1)}, bf16[16,18992]{1,0:T(8,128)(2,1)S(1)}, u32[]{:S(2)}, u32[]{:S(2)}) collective-permute-start(bf16[16,18992]{1,0:T(8,128)(2,1)S(1)} %get-tuple-element.122), channel_id=1, source_target_pairs={{0,4},{1,12},{2,20},{3,28},{4,0},{5,8},{6,16},{7,24},{8,5},{9,13},... | collective-permute-start | bytes 1823240 | tf_op jit(solution)/shard_map/ppermute | solution.py:76
  484.5 47.7 %collective-permute-start.13 = (bf16[16,18992]{1,0:T(8,128)(2,1)S(1)}, bf16[16,18992]{1,0:T(8,128)(2,1)S(1)}, u32[]{:S(2)}, u32[]{:S(2)}) collective-permute-start(bf16[16,18992]{1,0:T(8,128)(2,1)S(1)} %get-tuple-element.123), channel_id=1, source_target_pairs={{0,24},{1,0},{2,8},{3,16},{4,28},{5,4},{6,12},{7,20},{8,25},{9,1},... | collective-permute-start | bytes 1823240 | tf_op jit(solution)/shard_map/ppermute | solution.py:76
  490.0 43.5 %collective-permute-start.12 = (bf16[16,18992]{1,0:T(8,128)(2,1)S(1)}, bf16[16,18992]{1,0:T(8,128)(2,1)S(1)}, u32[]{:S(2)}, u32[]{:S(2)}) collective-permute-start(bf16[16,18992]{1,0:T(8,128)(2,1)S(1)} %get-tuple-element.124), channel_id=1, source_target_pairs={{0,16},{1,24},{2,0},{3,8},{4,20},{5,28},{6,4},{7,12},{8,17},{9,25}... | collective-permute-start | bytes 1823240 | tf_op jit(solution)/shard_map/ppermute | solution.py:76
  490.0 52.7 %collective-permute-start.11 = (bf16[16,18992]{1,0:T(8,128)(2,1)S(1)}, bf16[16,18992]{1,0:T(8,128)(2,1)S(1)}, u32[]{:S(2)}, u32[]{:S(2)}) collective-permute-start(bf16[16,18992]{1,0:T(8,128)(2,1)S(1)} %get-tuple-element.125), channel_id=1, source_target_pairs={{0,8},{1,16},{2,24},{3,0},{4,12},{5,20},{6,28},{7,4},{8,9},{9,17},... | collective-permute-start | bytes 1823240 | tf_op jit(solution)/shard_map/ppermute | solution.py:76
  497.8 70.9 %collective-permute-start.2 = (s16[64,9600]{1,0:T(8,128)(2,1)S(1)}, s16[64,9600]{1,0:T(8,128)(2,1)S(1)}, u32[]{:S(2)}, u32[]{:S(2)}) collective-permute-start(s16[64,9600]{1,0:T(8,128)(2,1)S(1)} %copy-done.8), channel_id=1, source_target_pairs={{0,8},{4,12},{8,16},{12,20},{1,9},{5,13},{9,17},{13,21},{2,10},{6,... | collective-permute-start | bytes 3686408 | tf_op jit(solution)/shard_map/ppermute | solution.py:108
  530.9 64.2 %collective-permute-start.20 = (s16[64,9600]{1,0:T(8,128)(2,1)}, s16[64,9600]{1,0:T(8,128)(2,1)}, u32[]{:S(2)}, u32[]{:S(2)}) collective-permute-start(s16[64,9600]{1,0:T(8,128)(2,1)} %fusion.31), channel_id=1, source_target_pairs={{0,8},{4,12},{8,16},{12,20},{1,9},{5,13},{9,17},{13,21},{2,10},{6,... | collective-permute-start | bytes 3686408 | tf_op jit(solution)/shard_map/ppermute | solution.py:108
  532.2 89.3 %collective-permute-start.27 = (s16[64,9600]{1,0:T(8,128)(2,1)}, s16[64,9600]{1,0:T(8,128)(2,1)}, u32[]{:S(2)}, u32[]{:S(2)}) collective-permute-start(s16[64,9600]{1,0:T(8,128)(2,1)} %fusion.37), channel_id=1, source_target_pairs={{0,8},{4,12},{8,16},{12,20},{1,9},{5,13},{9,17},{13,21},{2,10},{6,... | collective-permute-start | bytes 3686408 | tf_op jit(solution)/shard_map/ppermute | solution.py:108
  533.5 114.6 %collective-permute-start.34 = (s16[64,9696]{1,0:T(8,128)(2,1)S(1)}, s16[64,9696]{1,0:T(8,128)(2,1)}, u32[]{:S(2)}, u32[]{:S(2)}) collective-permute-start(s16[64,9696]{1,0:T(8,128)(2,1)S(1)} %fusion.17), channel_id=1, source_target_pairs={{0,8},{4,12},{8,16},{12,20},{1,9},{5,13},{9,17},{13,21},{2,10},{6,... | collective-permute-start | bytes 3723272 | tf_op jit(solution)/shard_map/ppermute | solution.py:108
  545.8 64.0 %slice-start.3 = ((s8[9699328]{0:T(1024)(128)(4,1)}), s8[1310720]{0:T(1024)(128)(4,1)S(1)}, s32[]{:S(2)}) async-start(s8[9699328]{0:T(1024)(128)(4,1)} %bitcast.501), calls=%async_computation.4 | async-start | bytes 2621440
  596.1 13.8 %slice-start.4 = ((s8[9699328]{0:T(1024)(128)(4,1)}), s8[4194304]{0:T(1024)(128)(4,1)S(1)}, s32[]{:S(2)}) async-start(s8[9699328]{0:T(1024)(128)(4,1)} %bitcast.501), calls=%async_computation.5 | async-start | bytes 8388608
  596.1 13.8 %slice-start.5 = ((s8[9699328]{0:T(1024)(128)(4,1)}), s8[4194304]{0:T(1024)(128)(4,1)S(1)}, s32[]{:S(2)}) async-start(s8[9699328]{0:T(1024)(128)(4,1)} %bitcast.501), calls=%async_computation.6 | async-start | bytes 8388608
  601.0 8.8 copy-start.10
  601.0 60.6 %collective-permute-start.22 = (s16[64,9600]{1,0:T(8,128)(2,1)}, s16[64,9600]{1,0:T(8,128)(2,1)}, u32[]{:S(2)}, u32[]{:S(2)}) collective-permute-start(s16[64,9600]{1,0:T(8,128)(2,1)} %fusion.33), channel_id=1, source_target_pairs={{28,20},{24,16},{29,21},{25,17},{30,22},{26,18},{31,23},{27,19}} | collective-permute-start | bytes 3686408 | tf_op jit(solution)/shard_map/ppermute | solution.py:109
  604.3 71.3 %collective-permute-start.21 = (s16[64,9600]{1,0:T(8,128)(2,1)}, s16[64,9600]{1,0:T(8,128)(2,1)}, u32[]{:S(2)}, u32[]{:S(2)}) collective-permute-start(s16[64,9600]{1,0:T(8,128)(2,1)} %fusion.32), channel_id=1, source_target_pairs={{0,8},{4,12},{8,16},{12,20},{16,24},{20,28},{1,9},{5,13},{9,17},{1... | collective-permute-start | bytes 3686408 | tf_op jit(solution)/shard_map/ppermute | solution.py:108
  610.7 46.1 %slice-start = ((s8[9830400]{0:T(1024)(128)(4,1)}), s8[1441792]{0:T(1024)(128)(4,1)S(1)}, s32[]{:S(2)}) async-start(s8[9830400]{0:T(1024)(128)(4,1)} %bitcast.493), calls=%async_computation.1 | async-start | bytes 2883584
  612.1 56.0 %collective-permute-start.4 = (s16[64,9600]{1,0:T(8,128)(2,1)}, s16[64,9600]{1,0:T(8,128)(2,1)}, u32[]{:S(2)}, u32[]{:S(2)}) collective-permute-start(s16[64,9600]{1,0:T(8,128)(2,1)} %fusion.27), channel_id=1, source_target_pairs={{28,20},{24,16},{29,21},{25,17},{30,22},{26,18},{31,23},{27,19}} | collective-permute-start | bytes 3686408 | tf_op jit(solution)/shard_map/ppermute | solution.py:109
  621.5 79.3 %collective-permute-start.3 = (s16[64,9600]{1,0:T(8,128)(2,1)}, s16[64,9600]{1,0:T(8,128)(2,1)}, u32[]{:S(2)}, u32[]{:S(2)}) collective-permute-start(s16[64,9600]{1,0:T(8,128)(2,1)} %fusion.26), channel_id=1, source_target_pairs={{0,8},{4,12},{8,16},{12,20},{16,24},{20,28},{1,9},{5,13},{9,17},{1... | collective-permute-start | bytes 3686408 | tf_op jit(solution)/shard_map/ppermute | solution.py:108
  649.1 7.7 slice-start.1
  654.1 51.1 %collective-permute-start.29 = (s16[64,9600]{1,0:T(8,128)(2,1)}, s16[64,9600]{1,0:T(8,128)(2,1)}, u32[]{:S(2)}, u32[]{:S(2)}) collective-permute-start(s16[64,9600]{1,0:T(8,128)(2,1)} %fusion.39), channel_id=1, source_target_pairs={{28,20},{24,16},{29,21},{25,17},{30,22},{26,18},{31,23},{27,19}} | collective-permute-start | bytes 3686408 | tf_op jit(solution)/shard_map/ppermute | solution.py:109
  661.6 65.5 %collective-permute-start.28 = (s16[64,9600]{1,0:T(8,128)(2,1)}, s16[64,9600]{1,0:T(8,128)(2,1)}, u32[]{:S(2)}, u32[]{:S(2)}) collective-permute-start(s16[64,9600]{1,0:T(8,128)(2,1)} %fusion.38), channel_id=1, source_target_pairs={{0,8},{4,12},{8,16},{12,20},{16,24},{20,28},{1,9},{5,13},{9,17},{1... | collective-permute-start | bytes 3686408 | tf_op jit(solution)/shard_map/ppermute | solution.py:108
  668.1 61.9 %collective-permute-start.36 = (s16[64,9696]{1,0:T(8,128)(2,1)}, s16[64,9696]{1,0:T(8,128)(2,1)}, u32[]{:S(2)}, u32[]{:S(2)}) collective-permute-start(s16[64,9696]{1,0:T(8,128)(2,1)} %fusion.19), channel_id=1, source_target_pairs={{28,20},{24,16},{29,21},{25,17},{30,22},{26,18},{31,23},{27,19}} | collective-permute-start | bytes 3723272 | tf_op jit(solution)/shard_map/ppermute | solution.py:109
  675.5 78.3 %collective-permute-start.35 = (s16[64,9696]{1,0:T(8,128)(2,1)}, s16[64,9696]{1,0:T(8,128)(2,1)}, u32[]{:S(2)}, u32[]{:S(2)}) collective-permute-start(s16[64,9696]{1,0:T(8,128)(2,1)} %fusion.18), channel_id=1, source_target_pairs={{0,8},{4,12},{8,16},{12,20},{16,24},{20,28},{1,9},{5,13},{9,17},{1... | collective-permute-start | bytes 3723272 | tf_op jit(solution)/shard_map/ppermute | solution.py:108
  700.8 53.9 %collective-permute-start.23 = (s16[64,9600]{1,0:T(8,128)(2,1)}, s16[64,9600]{1,0:T(8,128)(2,1)}, u32[]{:S(2)}, u32[]{:S(2)}) collective-permute-start(s16[64,9600]{1,0:T(8,128)(2,1)} %fusion.34), channel_id=1, source_target_pairs={{28,20},{24,16},{20,12},{16,8},{29,21},{25,17},{21,13},{17,9},{30,... | collective-permute-start | bytes 3686408 | tf_op jit(solution)/shard_map/ppermute | solution.py:109
  705.1 60.4 %collective-permute-start.5 = (s16[64,9600]{1,0:T(8,128)(2,1)}, s16[64,9600]{1,0:T(8,128)(2,1)}, u32[]{:S(2)}, u32[]{:S(2)}) collective-permute-start(s16[64,9600]{1,0:T(8,128)(2,1)} %fusion.28), channel_id=1, source_target_pairs={{28,20},{24,16},{20,12},{16,8},{29,21},{25,17},{21,13},{17,9},{30,... | collective-permute-start | bytes 3686408 | tf_op jit(solution)/shard_map/ppermute | solution.py:109
  727.2 64.7 %collective-permute-start.30 = (s16[64,9600]{1,0:T(8,128)(2,1)}, s16[64,9600]{1,0:T(8,128)(2,1)}, u32[]{:S(2)}, u32[]{:S(2)}) collective-permute-start(s16[64,9600]{1,0:T(8,128)(2,1)} %fusion.40), channel_id=1, source_target_pairs={{28,20},{24,16},{20,12},{16,8},{29,21},{25,17},{21,13},{17,9},{30,... | collective-permute-start | bytes 3686408 | tf_op jit(solution)/shard_map/ppermute | solution.py:109
  733.9 84.5 %collective-permute-start.37 = (s16[64,9696]{1,0:T(8,128)(2,1)S(1)}, s16[64,9696]{1,0:T(8,128)(2,1)S(1)}, u32[]{:S(2)}, u32[]{:S(2)}) collective-permute-start(s16[64,9696]{1,0:T(8,128)(2,1)S(1)} %fusion.20), channel_id=1, source_target_pairs={{28,20},{24,16},{20,12},{16,8},{29,21},{25,17},{21,13},{17,9},{30,... | collective-permute-start | bytes 3723272 | tf_op jit(solution)/shard_map/ppermute | solution.py:109
  759.7 85.1 %collective-permute-start.24 = (s16[64,9600]{1,0:T(8,128)(2,1)}, s16[64,9600]{1,0:T(8,128)(2,1)}, u32[]{:S(2)}, u32[]{:S(2)}) collective-permute-start(s16[64,9600]{1,0:T(8,128)(2,1)} %fusion.35), channel_id=1, source_target_pairs={{28,20},{24,16},{20,12},{16,8},{12,4},{8,0},{29,21},{25,17},{21,13... | collective-permute-start | bytes 3686408 | tf_op jit(solution)/shard_map/ppermute | solution.py:109
  770.4 100.8 %collective-permute-start.6 = (s16[64,9600]{1,0:T(8,128)(2,1)}, s16[64,9600]{1,0:T(8,128)(2,1)}, u32[]{:S(2)}, u32[]{:S(2)}) collective-permute-start(s16[64,9600]{1,0:T(8,128)(2,1)} %fusion.29), channel_id=1, source_target_pairs={{28,20},{24,16},{20,12},{16,8},{12,4},{8,0},{29,21},{25,17},{21,13... | collective-permute-start | bytes 3686408 | tf_op jit(solution)/shard_map/ppermute | solution.py:109
  796.8 100.8 %collective-permute-start.31 = (s16[64,9600]{1,0:T(8,128)(2,1)}, s16[64,9600]{1,0:T(8,128)(2,1)}, u32[]{:S(2)}, u32[]{:S(2)}) collective-permute-start(s16[64,9600]{1,0:T(8,128)(2,1)} %fusion.41), channel_id=1, source_target_pairs={{28,20},{24,16},{20,12},{16,8},{12,4},{8,0},{29,21},{25,17},{21,13... | collective-permute-start | bytes 3686408 | tf_op jit(solution)/shard_map/ppermute | solution.py:109
  822.3 101.0 %collective-permute-start.38 = (s16[64,9696]{1,0:T(8,128)(2,1)}, s16[64,9696]{1,0:T(8,128)(2,1)}, u32[]{:S(2)}, u32[]{:S(2)}) collective-permute-start(s16[64,9696]{1,0:T(8,128)(2,1)} %fusion.21), channel_id=1, source_target_pairs={{28,20},{24,16},{20,12},{16,8},{12,4},{8,0},{29,21},{25,17},{21,13... | collective-permute-start | bytes 3723272 | tf_op jit(solution)/shard_map/ppermute | solution.py:109
  875.6 26.5 %copy-start = (f32[64,9472]{1,0:T(8,128)}, f32[64,9472]{1,0:T(8,128)S(1)}, u32[]{:S(2)}) copy-start(f32[64,9472]{1,0:T(8,128)S(1)} %get-tuple-element.44) | copy-start | bytes 7274500
  (14 other events, 59.1 us)
Sparse Core Ops, SparseCore 0:
  9.6 27.7 all-gather.1
